TPU v7x, 1024 devices: a whole 4x4x32 slice. The times are simulated.
1024 devices in a mesh: section: 4 (over y), head: 8 (over x, core), tok: 32 (over z).
Axes of the slice: x: 4, y: 4, z: 32, core: 2. Of those that a mesh axis runs over, the one named last changes fastest.
Arguments:
- queries: bfloat16 [12288, 4096], P('tok', 'head'), may hold values from -10 to 10
- key_values: bfloat16 [32, 4, 96, 8, 256], P('tok', 'section', None, 'head'), may hold values from -10 to 10
- lengths: int32 [8], replicated, may hold values from 1 to 6144, 12288 in all
Outputs:
- attended: bfloat16 [12288, 4096], P('tok', 'head')
All inputs are finite; a program needn't handle non-finite values.
Results may differ from a plain program's by a relative error of at most 0.0055.
Values may be sent and summed in bfloat16 or wider, within the bound.
No kernel may reach another device: no remote copies, remote signals or barrier semaphores. Data moves between devices by JAX's collectives and lax.ppermute only.
A program may use at most 32 MiB of HBM per device.

v0:
```python
import jax
import jax.numpy as jnp
from jax import lax
from jax.sharding import PartitionSpec as P


def joined(value, axis, join):
    pieces = jax.tree.map(lambda part: lax.all_gather(part, axis), value)
    head = jax.tree.map(lambda part: part[0], pieces)
    tail = jax.tree.map(lambda part: part[1:], pieces)
    total, _ = lax.scan(lambda total, slab: (join(total, slab), None), head, tail)
    return total


def doc_index(positions, ends):
    return jnp.sum((positions[:, None] >= ends[None, :]).astype(jnp.int32), axis=1)


def doc_begin(positions, ends):
    return jnp.max(
        jnp.where(ends[None, :] <= positions[:, None], ends[None, :], jnp.int32(0)), axis=1
    )


def combine_parts(first, second):
    peak = jnp.maximum(first[0], second[0])
    scale_one = jnp.exp(first[0] - peak)
    scale_two = jnp.exp(second[0] - peak)
    total = first[1] * scale_one + second[1] * scale_two
    sums = first[2] * scale_one[..., None] + second[2] * scale_two[..., None]
    return (peak, total, sums)


def update_state(state, query_half, query_pos, query_doc, keys, values, key_pos, key_doc, scale):
    peak_old, total_old, sums_old = state
    scores = (
        jnp.einsum("rgjd,kgd->rgjk", query_half, keys, preferred_element_type=jnp.float32) * scale
    )
    visible = (key_pos[None, :] <= query_pos[:, None]) & (key_doc[None, :] == query_doc[:, None])
    visible = visible[:, None, None, :]
    scores = jnp.where(visible, scores, jnp.float32(-1e30))
    peak_new = jnp.maximum(peak_old, jnp.max(scores, axis=-1))
    weights = jnp.where(visible, jnp.exp(scores - peak_new[..., None]), jnp.float32(0.0))
    factor = jnp.exp(peak_old - peak_new)
    total_new = total_old * factor + jnp.sum(weights, axis=-1)
    mixed = jnp.einsum(
        "rgjk,kgd->rgjd", weights.astype(jnp.bfloat16), values, preferred_element_type=jnp.float32
    )
    return (peak_new, total_new, sums_old * factor[..., None] + mixed)


def keep_state(state):
    return state


def shards(queries, key_values, lengths):
    rows = queries.shape[0]
    width = queries.shape[1]
    heads_kv = key_values.shape[3]
    head_size = key_values.shape[4] // 2
    group = width // (heads_kv * head_size)
    key_rows = key_values.shape[2]
    scale = head_size ** (-0.5)
    tile = lax.axis_index("tok")
    split = lax.axis_index("section")
    ends = jnp.cumsum(lengths)
    positions = tile * rows + jnp.arange(rows, dtype=jnp.int32)
    half = rows // 2
    query_heads = queries.reshape(rows, heads_kv, group, head_size)
    halves = []
    initial = []
    for half_index in range(2):
        lower = half_index * half
        half_pos = positions[lower : lower + half]
        halves.append(
            (
                query_heads[lower : lower + half],
                half_pos,
                doc_index(half_pos, ends),
                jnp.max(half_pos),
                jnp.min(doc_begin(half_pos, ends)),
            )
        )
        initial.append(
            (
                jnp.full((half, heads_kv, group), -1e30, jnp.float32),
                jnp.zeros((half, heads_kv, group), jnp.float32),
                jnp.zeros((half, heads_kv, group, head_size), jnp.float32),
            )
        )
    piece = lax.all_gather(key_values, "tok", axis=0, tiled=True)
    count = piece.shape[0]
    flat = piece.reshape(count, key_rows, heads_kv, 2 * head_size)
    bunch = min(4, count)
    whole_steps = count // bunch

    def some_tiles(first_tile, number, state):
        block = lax.dynamic_slice_in_dim(flat, first_tile, number, 0).reshape(
            number * key_rows, heads_kv, 2 * head_size
        )
        keys = block[:, :, :head_size]
        values = block[:, :, head_size:]
        tile_ids = first_tile + jnp.arange(number, dtype=jnp.int32)
        key_pos = (
            tile_ids[:, None] * rows
            + split * key_rows
            + jnp.arange(key_rows, dtype=jnp.int32)[None, :]
        ).reshape(number * key_rows)
        key_doc = doc_index(key_pos, ends)
        lowest = jnp.min(key_pos)
        highest = jnp.max(key_pos)
        updated = []
        for details, current in zip(halves, state):
            query_half, query_pos, query_doc, last_pos, begin = details
            live = (lowest <= last_pos) & (highest >= begin)

            def apply_update(old_state):
                return update_state(
                    old_state,
                    query_half,
                    query_pos,
                    query_doc,
                    keys,
                    values,
                    key_pos,
                    key_doc,
                    scale,
                )

            updated.append(lax.cond(live, apply_update, keep_state, current))
        return tuple(updated)

    def step_tiles(index, state):
        return some_tiles(index * bunch, bunch, state)

    result = lax.fori_loop(0, whole_steps, step_tiles, tuple(initial))
    peaks = jnp.concatenate([result[0][0], result[1][0]], axis=0)
    totals = jnp.concatenate([result[0][1], result[1][1]], axis=0)
    sums = jnp.concatenate([result[0][2], result[1][2]], axis=0)
    peaks, totals, sums = joined((peaks, totals, sums), "section", combine_parts)
    finished = (sums / totals[..., None]).astype(jnp.bfloat16).reshape(rows, width)
    return finished


def solution(mesh):
    return jax.shard_map(
        shards,
        mesh=mesh,
        in_specs=(P("tok", "head"), P("tok", "section", None, "head", None), P()),
        out_specs=P("tok", "head"),
        check_vma=False,
    )
```

profile of v0, /device:TPU:6, one launch (start us, length us, event | category | flops | bytes accessed | tf_op | source)
XLA Modules:
  0.0 294.5 jit_solution(11550851120962788542)
XLA Ops:
  10.3 1.0 fusion.40
  11.5 144.0 %all-gather.6.cloned.1.call-done = bf16[32,1,96,1,256]{4,2,3,1,0:T(8,128)(2,1)} async-done(((bf16[1,1,96,1,256]{4,2,3,1,0:T(8,128)(2,1)}), bf16[32,1,96,1,256]{4,2,3,1,0:T(8,128)(2,1)}) %all-gather.6.cloned.1.call-update) | async-done | bytes 1572880 | tf_op jit(solution)/shard_map/all_gather | solution.py:91
  155.7 60.1 %while.39 = (s32[]{:T(128)}, f32[192,1,4]{0,2,1:T(4,128)S(1)}, f32[192,1,4]{0,2,1:T(4,128)S(1)}, f32[192,1,4,128]{3,0,2,1:T(8,128)S(1)}, f32[192,1,4]{0,2,1:T(4,...) while((s32[]{:T(128)}, f32[192,1,4]{0,2,1:T(4,128)S(1)}, ...), condition=%wide.region_21.22_spmd, body=%wide.region_9.21_spmd.sunk | while | flops 308148480 | bytes 10935451 | solution.py:136
  155.7 0.9 constant_dynamic-slice_fusion.2
  160.1 1.7 conditional.5
  164.4 1.7 conditional.4
  173.3 0.9 constant_dynamic-slice_fusion.2
  180.4 0.9 constant_dynamic-slice_fusion.2
  216.3 1.1 pad_maximum_fusion
  217.5 11.9 %all-gather.1 = f32[1536,1,4]{0,2,1:T(4,128)S(1)} all-gather(f32[384,1,4]{0,2,1:T(4,128)S(1)} %pad_maximum_fusion.2), channel_id=3, replica_groups=mesh['section'=4,'head'=8,'tok'=32] {'section'}, dimensions={0}, use_global_device_ids=true | all-gather | bytes 30720 | tf_op jit(solution)/shard_map/all_gather | solution.py:8
  230.7 11.9 %all-gather = f32[1536,1,4]{0,2,1:T(4,128)S(1)} all-gather(f32[384,1,4]{0,2,1:T(4,128)S(1)} %pad_maximum_fusion.1), channel_id=2, replica_groups=mesh['section'=4,'head'=8,'tok'=32] {'section'}, dimensions={0}, use_global_device_ids=true | all-gather | bytes 30720 | tf_op jit(solution)/shard_map/all_gather | solution.py:8
  243.2 24.3 %all-gather.8.cloned.1.call-done = f32[1536,1,4,128]{3,2,1,0:T(4,128)} async-done(((f32[384,1,4,128]{3,2,1,0:T(4,128)}), f32[1536,1,4,128]{3,2,1,0:T(4,128)}) %all-gather.8.cloned.1.call-update) | async-done | bytes 3145744 | tf_op jit(solution)/shard_map/all_gather | solution.py:8
  267.5 1.7 slice.79
  269.2 1.1 slice-done
  270.3 15.2 %while.40 = (s32[]{:T(128)}, f32[384,1,4]{0,2,1:T(4,128)S(1)}, f32[384,1,4]{0,2,1:T(4,128)}, f32[384,1,4,128]{3,2,1,0:T(4,128)S(1)}, f32[3,384,1,4]{1,3,2,0:T(4,...) while((s32[]{:T(128)}, f32[384,1,4]{0,2,1:T(4,128)S(1)}, ...), condition=%wide.region_23.24_spmd, body=%wide.region_22.23_spmd.sunk | while | flops 600578 | bytes 2476129 | solution.py:11
  270.3 1.3 fusion.48
  271.6 1.3 fusion.49
  273.9 1.4 fusion.50
  275.4 1.3 fusion.48
  276.7 1.3 fusion.49
  279.0 1.4 fusion.50
  280.4 1.3 fusion.48
  281.7 1.3 fusion.49
  284.1 1.4 fusion.50
  (116 shorter events, 27.6 us)
Async XLA Ops:
  6.5 149.0 %all-gather.6.cloned.1.call-start = ((), (), s32[]{:S(2)}) async-start(), calls=%async_computation | async-start | bytes 1622016 | tf_op jit(solution)/shard_map/all_gather | solution.py:91
  7.3 260.2 %all-gather.8.cloned.1.call-start = ((), (), s32[]{:S(2)}) async-start(), calls=%async_computation.1 | async-start | bytes 3932160 | tf_op jit(solution)/shard_map/all_gather | solution.py:8
  269.2 1.1 slice-start
Sparse Core Ops, SparseCore 0:
  10.0 145.4 all-gather.5
  217.5 49.9 all-gather.7
where the time goes:
time: 297 us; the launch traced here: 294 us
  waiting for transfers between devices  169 us (57%)
  loops' own time  41.5 us (14%)
  other arithmetic  25.2 us (8%)
  blocking collectives  23.8 us (8%)
  local copies, waits for them, and re-layouts  19.5 us (7%)
  between operations  13.5 us (5%)
    all_gather x1, waiting for transfers between devices, shards(): piece = lax.all_gather(key_values, 'tok', axis=0, tiled=True)  144 us
    another operation x1, loops' own time, shards(): result = lax.fori_loop(0, whole_steps, step_tiles, tuple(initial))  41.1 us
    all_gather x1, waiting for transfers between devices, joined(): pieces = jax.tree.map(lambda part: lax.all_gather(part, axis), value)  24.3 us
    all_gather x2, blocking collectives, joined(): pieces = jax.tree.map(lambda part: lax.all_gather(part, axis), value)  23.8 us
    mul x6, other arithmetic, combine_parts(): sums = first[2] * scale_one[..., None] + second[2] * scale_two[..., None]  7.89 us
    dynamic_slice x8, local copies, waits for them, and re-layouts, some_tiles(): lax.dynamic_slice_in_dim(flat, first_tile, number, 0)  7.56 us
    reduce_max x8, other arithmetic, some_tiles(): highest = jnp.max(key_pos)  6.27 us
  transfers between devices with their start and end apart: 2, of which 2 were waited for; matrix products, arithmetic and copies ran while one was open for 2% of the time, Pallas kernels for 0%

commit v1 on v0

v1 whole, which is shorter than its diff:
```python
import functools
import math

import jax
import jax.numpy as jnp
from jax import lax
from jax.experimental import pallas as pl
from jax.experimental.pallas import tpu as pltpu
from jax.sharding import PartitionSpec as P

LOW = -1e30
FLOOR = -5e29
LANES = 128
NDOCS = 8
STAT_ROWS = 32
WHOLE = pl.BlockSpec(memory_space=pltpu.VMEM)
SCALARS = pl.BlockSpec(memory_space=pltpu.SMEM)
EARLY = ((0,), (4,), (2, 6), (1, 5, 3, 7), (8,), (12,))
LATE = ((10, 14), (9, 13, 11, 15), (16,))


def shift(value, axis, by, count):
    return lax.ppermute(value, axis, [(i, (i + by) % count) for i in range(count)])


def query_bounds(info, rows):
    place = info[0] * rows + lax.broadcasted_iota(jnp.int32, (rows, LANES), 0)
    begin = jnp.zeros((rows, LANES), jnp.int32)
    end = jnp.int32(0)
    for i in range(NDOCS):
        end = end + info[2 + i]
        begin = jnp.where(end <= place, end, begin)
    return place[:, :1], begin[:, :1]


def key_places(info, rows, key_rows, distances):
    parts = []
    for d in distances:
        base = (info[0] - d) * rows + info[1] * key_rows
        parts.append(base + lax.broadcasted_iota(jnp.int32, (1, key_rows), 1))
    return jnp.concatenate(parts, axis=1)


def scores_of(query, keys):
    return lax.dot_general(
        query, keys, (((1,), (1,)), ((), ())), preferred_element_type=jnp.float32
    )


def attend(factor, query, keys, values, visible, peak, total, sums):
    scores = jnp.where(visible, scores_of(query, keys), LOW)
    top = jnp.maximum(peak, jnp.max(scores, axis=1, keepdims=True))
    weights = jnp.exp2((scores - top) * factor).astype(jnp.bfloat16)
    mixed = jnp.dot(weights, values, preferred_element_type=jnp.float32)
    decay = jnp.exp2((peak - top) * factor)
    size = sums.shape[1]
    return top, total * decay + mixed[:, size : size + 1], sums * decay + mixed[:, :size]


def gathered(refs, size):
    keys = jnp.concatenate([ref[:, :size] for ref in refs], axis=0)
    values = jnp.concatenate([ref[:, size:] for ref in refs], axis=0)
    ones = jnp.ones((values.shape[0], LANES), values.dtype)
    return keys, jnp.concatenate([values, ones], axis=1)


def pack_stats(peaks, totals, rows):
    lane = lax.broadcasted_iota(jnp.int32, (rows, LANES), 1)
    stats = jnp.zeros((rows, LANES), jnp.float32)
    count = len(peaks)
    for h in range(count):
        stats = jnp.where(lane == h, peaks[h], stats)
        stats = jnp.where(lane == 4 + h, totals[h], stats)
    return stats


def early_kernel(factor, size, key_rows, info, q_ref, *refs):
    *kv_refs, sums_ref, stats_ref = refs
    rows = q_ref.shape[0]
    heads = q_ref.shape[1] // size
    place, begin = query_bounds(info, rows)
    own_keys, own_values = gathered(kv_refs[:1], size)
    own_place = key_places(info, rows, key_rows, EARLY[0])
    own_visible = (own_place <= place) & (own_place >= begin)
    keys, values = gathered(kv_refs[1:], size)
    distances = [d for group in EARLY[1:] for d in group]
    visible = key_places(info, rows, key_rows, distances) >= begin
    peaks, totals = [], []
    for h in range(heads):
        cols = slice(h * size, (h + 1) * size)
        query = q_ref[:, cols]
        state = (
            jnp.full((rows, 1), FLOOR, jnp.float32),
            jnp.zeros((rows, 1), jnp.float32),
            jnp.zeros((rows, size), jnp.float32),
        )
        state = attend(factor, query, own_keys, own_values, own_visible, *state)
        state = attend(factor, query, keys, values, visible, *state)
        peaks.append(state[0])
        totals.append(state[1])
        sums_ref[:, cols] = state[2]
    stats_ref[...] = pack_stats(peaks, totals, rows)


def late_kernel(factor, size, key_rows, info, q_ref, sums_ref, stats_ref, *refs):
    *kv_refs, out_ref = refs
    rows = q_ref.shape[0]
    width = q_ref.shape[1]
    heads = width // size
    _, begin = query_bounds(info, rows)
    keys, values = gathered(kv_refs, size)
    distances = [d for group in LATE for d in group]
    visible = key_places(info, rows, key_rows, distances) >= begin
    peaks, totals = [], []
    for h in range(heads):
        cols = slice(h * size, (h + 1) * size)
        state = (stats_ref[:, h : h + 1], stats_ref[:, 4 + h : 5 + h], sums_ref[:, cols])
        state = attend(factor, q_ref[:, cols], keys, values, visible, *state)
        peaks.append(state[0])
        totals.append(state[1])
        out_ref[:rows, cols] = state[2].astype(jnp.bfloat16)
    stats = jnp.transpose(pack_stats(peaks, totals, rows))[:8]
    high = stats.astype(jnp.bfloat16).astype(jnp.float32)
    rest = stats - high
    middle = rest.astype(jnp.bfloat16).astype(jnp.float32)
    low = rest - middle
    packed = jnp.concatenate([high, middle, low, jnp.zeros_like(low)], axis=0)
    spare = jnp.zeros((STAT_ROWS, width - rows), jnp.float32)
    out_ref[rows:, :] = jnp.concatenate([packed, spare], axis=1).astype(jnp.bfloat16)


def merge_kernel(factor, size, *refs):
    *parts, out_ref = refs
    rows = out_ref.shape[0]
    heads = out_ref.shape[1] // size
    peaks, totals = [], []
    for part in parts:
        packed = part[rows:, :].astype(jnp.float32)[:, :rows]
        stats = packed[0:8] + packed[8:16] + packed[16:24]
        peaks.append(stats)
        totals.append(pltpu.roll(stats, 4, 0))
    top = functools.reduce(jnp.maximum, peaks)
    scaled = [jnp.exp2(jnp.minimum((peak - top) * factor, 0.0)) for peak in peaks]
    terms = [s * t for s, t in zip(scaled, totals)]
    total = (terms[0] + terms[2]) + (terms[1] + terms[3])
    shares = [s / total for s in scaled]
    blank = jnp.zeros((LANES - 8 * len(parts), rows), jnp.float32)
    shares = jnp.transpose(jnp.concatenate(shares + [blank], axis=0))
    for h in range(heads):
        cols = slice(h * size, (h + 1) * size)
        terms = [
            part[:rows, cols].astype(jnp.float32) * shares[:, 8 * i + h : 8 * i + h + 1]
            for i, part in enumerate(parts)
        ]
        out_ref[:, cols] = ((terms[0] + terms[2]) + (terms[1] + terms[3])).astype(jnp.bfloat16)


def params():
    return pltpu.CompilerParams(vmem_limit_bytes=40 * 1024 * 1024)


def cost(rows, heads, keys, size):
    pairs = rows * heads * keys
    return pl.CostEstimate(
        flops=4 * pairs * size, bytes_accessed=2 * rows * heads * size, transcendentals=pairs
    )


def early_call(factor, size, key_rows, info, queries, chunks):
    rows, width = queries.shape
    return pl.pallas_call(
        functools.partial(early_kernel, factor, size, key_rows),
        out_shape=(
            jax.ShapeDtypeStruct((rows, width), jnp.float32),
            jax.ShapeDtypeStruct((rows, LANES), jnp.float32),
        ),
        in_specs=[SCALARS] + [WHOLE] * (1 + len(chunks)),
        out_specs=(WHOLE, WHOLE),
        compiler_params=params(),
        cost_estimate=cost(rows, width // size, 10 * key_rows, size),
        name="early",
    )(info, queries, *chunks)


def late_call(factor, size, key_rows, info, queries, state, chunks):
    rows, width = queries.shape
    return pl.pallas_call(
        functools.partial(late_kernel, factor, size, key_rows),
        out_shape=jax.ShapeDtypeStruct((rows + STAT_ROWS, width), jnp.bfloat16),
        in_specs=[SCALARS] + [WHOLE] * (3 + len(chunks)),
        out_specs=WHOLE,
        compiler_params=params(),
        cost_estimate=cost(rows, width // size, 7 * key_rows, size),
        name="late",
    )(info, queries, *state, *chunks)


def merge_call(factor, size, rows, parts):
    width = parts[0].shape[1]
    return pl.pallas_call(
        functools.partial(merge_kernel, factor, size),
        out_shape=jax.ShapeDtypeStruct((rows, width), jnp.bfloat16),
        in_specs=[WHOLE] * len(parts),
        out_specs=WHOLE,
        compiler_params=params(),
        name="merge",
    )(*parts)


def shards(tiles, splits, queries, key_values, lengths):
    rows = queries.shape[0]
    key_rows = key_values.shape[2]
    size = key_values.shape[4] // 2
    factor = size ** (-0.5) * math.log2(math.e)
    place = jnp.stack([lax.axis_index("tok"), lax.axis_index("section")]).astype(jnp.int32)
    info = jnp.concatenate([place, lengths])
    own = key_values.reshape(key_rows, 2 * size)
    along = lambda value, by: shift(value, "tok", by, tiles)
    far = along(own, 8)
    near4 = along(own, 4)
    near2 = along(jnp.concatenate([own, near4]), 2)
    far4 = along(far, 4)
    near1 = along(jnp.concatenate([own, near4, near2]), 1)
    far2 = along(jnp.concatenate([far, far4]), 2)
    far1 = along(jnp.concatenate([far, far4, far2]), 1)
    last = along(far2[key_rows:], 2)
    state = early_call(
        factor, size, key_rows, info, queries, (own, near4, near2, near1, far, far4)
    )
    part = late_call(factor, size, key_rows, info, queries, state, (far2, far1, last))
    parts = [part] + [shift(part, "section", by, splits) for by in range(1, splits)]
    return merge_call(factor, size, rows, parts)


def solution(mesh):
    return jax.shard_map(
        functools.partial(shards, mesh.shape["tok"], mesh.shape["section"]),
        mesh=mesh,
        in_specs=(P("tok", "head"), P("tok", "section", None, "head", None), P()),
        out_specs=P("tok", "head"),
        check_vma=False,
    )
```

time: 297 us -> 97.3 us (0.33)
  waiting for transfers between devices: 169 us -> 15.6 us
  starting transfers between devices: 0.04 us -> 70.1 us
  loops' own time: 41.5 us -> 0 us
  other arithmetic: 25.2 us -> 0.92 us
  blocking collectives: 23.8 us -> 0 us
  local copies, waits for them, and re-layouts: 19.5 us -> 0.66 us
  between operations: 13.5 us -> 0.17 us
  Pallas kernels: 0 us -> 9.08 us
    all_gather x2 -> x0, waiting for transfers between devices: 168 us -> none  [the longest x1 144 us: shards(): piece = lax.all_gather(key_values, 'tok', axis=0, tiled=True)]
    ppermute x0 -> x11, starting transfers between devices: none -> 70.1 us  [shift(): lax.ppermute(value, axis, [(i, (i + by) % count) for i in range(count)])]
    another operation x18 -> x0, loops' own time: 41.5 us -> none  [the longest x1 41.1 us: shards(): result = lax.fori_loop(0, whole_steps, step_tiles, tuple(initial))]
    all_gather x2 -> x0, blocking collectives: 23.8 us -> none  [joined(): pieces = jax.tree.map(lambda part: lax.all_gather(part, axis), value)]
    ppermute x0 -> x11, waiting for transfers between devices: none -> 15.6 us  [shift(): lax.ppermute(value, axis, [(i, (i + by) % count) for i in range(count)])]
    pallas_call x0 -> x3, Pallas kernels: none -> 9.08 us  [the longest x1 3.89 us: early_call(): pl.pallas_call(functools.partial(early_kernel, factor, size, key_rows), o...]
    mul x8 -> x0, other arithmetic: 7.91 us -> none  [the longest x6 7.89 us: combine_parts(): sums = first[2] * scale_one[..., None] + second[2] * scale_two[..., None]]
    dynamic_slice x8 -> x0, local copies, waits for them, and re-layouts: 7.56 us -> none  [some_tiles(): lax.dynamic_slice_in_dim(flat, first_tile, number, 0)]
  transfers between devices with their start and end apart: 2 -> 11, of which waited for: 2 -> 7; matrix products, arithmetic and copies ran while one was open for 2% -> 1% of each run, Pallas kernels for 0% -> 4%
where the time goes in v1:
time: 97.3 us; the launch traced here: 96.5 us
  starting transfers between devices  70.1 us (72%)
  waiting for transfers between devices  15.6 us (16%)
  Pallas kernels  9.08 us (9%)
    ppermute x11, starting transfers between devices, shift(): lax.ppermute(value, axis, [(i, (i + by) % count) for i in range(count)])  70.1 us
    ppermute x11, waiting for transfers between devices, shift(): lax.ppermute(value, axis, [(i, (i + by) % count) for i in range(count)])  15.6 us
    pallas_call x1, Pallas kernels, early_call(): pl.pallas_call(functools.partial(early_kernel, factor, size, key_rows), o...  3.89 us
    pallas_call x1, Pallas kernels, late_call(): pl.pallas_call(functools.partial(late_kernel, factor, size, key_rows), ou...  3.34 us
  transfers between devices with their start and end apart: 11, of which 7 were waited for; matrix products, arithmetic and copies ran while one was open for 1% of the time, Pallas kernels for 4%

profile of v1, /device:TPU:6, one launch (start us, length us, event | category | flops | bytes accessed | tf_op | source)
XLA Modules:
  0.0 96.5 jit_solution(10021593145139681311)
XLA Ops:
  0.0 15.7 %collective-permute-start.3 = (bf16[96,256]{1,0:T(8,128)(2,1)}, bf16[96,256]{1,0:T(8,128)(2,1)S(1)}, u32[]{:S(2)}, u32[]{:S(2)}) collective-permute-start(bf16[96,256]{1,0:T(8,128)(2,1)} %bitcast.3), channel_id=1, source_target_pairs={{0,8},{1,9},{2,10},{3,11},{4,12},{5,13},{6,14},{7,15},{8,16},{9,17... | collective-permute-start | bytes 147464 | tf_op jit(solution)/shard_map/ppermute | solution.py:23
  15.7 9.1 %collective-permute-start = (bf16[96,256]{1,0:T(8,128)(2,1)}, bf16[96,256]{1,0:T(8,128)(2,1)S(1)}, u32[]{:S(2)}, u32[]{:S(2)}) collective-permute-start(bf16[96,256]{1,0:T(8,128)(2,1)} %bitcast.4), channel_id=1, source_target_pairs={{0,4},{1,5},{2,6},{3,7},{4,8},{5,9},{6,10},{7,11},{8,12},{9,13},{1... | collective-permute-start | bytes 147464 | tf_op jit(solution)/shard_map/ppermute | solution.py:23
  24.8 0.8 collective-permute-done.3.refs_4_
  25.6 8.3 %collective-permute-start.4 = (bf16[96,256]{1,0:T(8,128)(2,1)S(1)}, bf16[96,256]{1,0:T(8,128)(2,1)S(1)}, u32[]{:S(2)}, u32[]{:S(2)}) collective-permute-start(bf16[96,256]{1,0:T(8,128)(2,1)S(1)} %collective-permute-done.3.refs_4_), channel_id=1, source_target_pairs={{0,4},{1,5},{2,6},{3,7},{4,8},{5,9},{6,10},{7,11},{8,12},{9,13},{1... | collective-permute-start | bytes 147464 | tf_op jit(solution)/shard_map/ppermute | solution.py:23
  34.0 0.8 pad_maximum_fusion.2
  34.8 8.5 %collective-permute-start.1 = (bf16[192,256]{1,0:T(8,128)(2,1)S(1)}, bf16[192,256]{1,0:T(8,128)(2,1)S(1)}, u32[]{:S(2)}, u32[]{:S(2)}) collective-permute-start(bf16[192,256]{1,0:T(8,128)(2,1)S(1)} %pad_maximum_fusion.2), channel_id=1, source_target_pairs={{0,2},{1,3},{2,4},{3,5},{4,6},{5,7},{6,8},{7,9},{8,10},{9,11},{10,... | collective-permute-start | bytes 294920 | tf_op jit(solution)/shard_map/ppermute | solution.py:23
  43.3 6.8 %collective-permute-start.5 = (bf16[192,256]{1,0:T(8,128)(2,1)S(1)}, bf16[192,256]{1,0:T(8,128)(2,1)S(1)}, u32[]{:S(2)}, u32[]{:S(2)}) collective-permute-start(bf16[192,256]{1,0:T(8,128)(2,1)S(1)} %pad_maximum_fusion.3), channel_id=1, source_target_pairs={{0,2},{1,3},{2,4},{3,5},{4,6},{5,7},{6,8},{7,9},{8,10},{9,11},{10,... | collective-permute-start | bytes 294920 | tf_op jit(solution)/shard_map/ppermute | solution.py:23
  50.2 0.5 collective-permute-done.1.refs_2_
  50.7 4.0 %collective-permute-start.2 = (bf16[384,256]{1,0:T(8,128)(2,1)S(1)}, bf16[384,256]{1,0:T(8,128)(2,1)S(1)}, u32[]{:S(2)}, u32[]{:S(2)}) collective-permute-start(bf16[384,256]{1,0:T(8,128)(2,1)S(1)} %pad_maximum_fusion), channel_id=1, source_target_pairs={{0,1},{1,2},{2,3},{3,4},{4,5},{5,6},{6,7},{7,8},{8,9},{9,10},{10,1... | collective-permute-start | bytes 589832 | tf_op jit(solution)/shard_map/ppermute | solution.py:23
  54.6 1.4 %collective-permute-done.5.refs_0_ = bf16[192,256]{1,0:T(8,128)(2,1)S(1)} collective-permute-done((bf16[192,256]{1,0:T(8,128)(2,1)S(1)}, bf16[192,256]{1,0:T(8,128)(2,1)S(1)}, u32[]{:S(2)}, u32[]{:S(2)}) %collective-permute-start.5) | collective-permute-done | bytes 98336 | tf_op jit(solution)/shard_map/ppermute | solution.py:23
  56.0 5.5 %collective-permute-start.6 = (bf16[384,256]{1,0:T(8,128)(2,1)S(1)}, bf16[384,256]{1,0:T(8,128)(2,1)S(1)}, u32[]{:S(2)}, u32[]{:S(2)}) collective-permute-start(bf16[384,256]{1,0:T(8,128)(2,1)S(1)} %pad_maximum_fusion.1), channel_id=1, source_target_pairs={{0,1},{1,2},{2,3},{3,4},{4,5},{5,6},{6,7},{7,8},{8,9},{9,10},{10,1... | collective-permute-start | bytes 589832 | tf_op jit(solution)/shard_map/ppermute | solution.py:23
  61.5 0.6 copy-done.2
  62.2 0.1 pad_add_fusion.info
  62.2 1.9 %collective-permute-start.7 = (bf16[96,256]{1,0:T(8,128)(2,1)S(1)}, bf16[96,256]{1,0:T(8,128)(2,1)S(1)}, u32[]{:S(2)}, u32[]{:S(2)}) collective-permute-start(bf16[96,256]{1,0:T(8,128)(2,1)S(1)} %slice.4), channel_id=1, source_target_pairs={{0,2},{1,3},{2,4},{3,5},{4,6},{5,7},{6,8},{7,9},{8,10},{9,11},{10,... | collective-permute-start | bytes 147464 | tf_op jit(solution)/shard_map/ppermute | solution.py:23
  64.2 3.9 %early.1 = (f32[384,512]{1,0:T(8,128)S(1)}, f32[384,128]{1,0:T(8,128)S(1)}) custom-call(s32[10]{0:T(128)S(1)} %pad_add_fusion.info, bf16[384,512]{1,0:T(8,128)(2,1)S(1)} %copy-done, bf16[96,256]{1,0:T(8,128)(2,1)S(1)} %bitcast.7, bf16[96,256]{1,0:T(8,128)(2,1)S(1)} %collective-permute-done.refs_1_, bf16[192,256]{1,0:T(8,128)(2,1)S(1)} %collective-permute-done.1.refs_2_, ...), custom_call_target="tpu_custom_call" | custom-call | flops 754974720 | bytes 393216 | tf_op jit(solution)/shard_map/early/pallas_call | solution.py:171
  68.1 2.3 %collective-permute-done.7.refs_2_ = bf16[96,256]{1,0:T(8,128)(2,1)S(1)} collective-permute-done((bf16[96,256]{1,0:T(8,128)(2,1)S(1)}, bf16[96,256]{1,0:T(8,128)(2,1)S(1)}, u32[]{:S(2)}, u32[]{:S(2)}) %collective-permute-start.7) | collective-permute-done | bytes 49184 | tf_op jit(solution)/shard_map/ppermute | solution.py:23
  70.3 3.3 %late.1.refs_0_ = bf16[416,512]{1,0:T(8,128)(2,1)S(1)} custom-call(s32[10]{0:T(128)S(1)} %pad_add_fusion.info, bf16[384,512]{1,0:T(8,128)(2,1)S(1)} %copy-done, f32[384,512]{1,0:T(8,128)S(1)} %get-tuple-element.7.sums_ref, f32[384,128]{1,0:T(8,128)S(1)} %get-tuple-element.8.stats_ref, bf16[192,256]{1,0:T(8,128)(2,1)S(1)} %collective-permute-done.5.refs_0_, ...), custom_call_target="tpu_custom_call" | custom-call | flops 528482304 | bytes 393216 | tf_op jit(solution)/shard_map/late/pallas_call | solution.py:187
  73.7 4.9 %collective-permute-start.10 = (bf16[416,512]{1,0:T(8,128)(2,1)S(1)}, bf16[416,512]{1,0:T(8,128)(2,1)S(1)}, u32[]{:S(2)}, u32[]{:S(2)}) collective-permute-start(bf16[416,512]{1,0:T(8,128)(2,1)S(1)} %late.1.refs_0_), channel_id=1, source_target_pairs={{0,768},{256,0},{512,256},{768,512},{1,769},{257,1},{513,257},{769... | collective-permute-start | bytes 1277960 | tf_op jit(solution)/shard_map/ppermute | solution.py:23
  78.6 2.5 %collective-permute-start.9 = (bf16[416,512]{1,0:T(8,128)(2,1)S(1)}, bf16[416,512]{1,0:T(8,128)(2,1)S(1)}, u32[]{:S(2)}, u32[]{:S(2)}) collective-permute-start(bf16[416,512]{1,0:T(8,128)(2,1)S(1)} %late.1.refs_0_), channel_id=1, source_target_pairs={{0,512},{256,768},{512,0},{768,256},{1,513},{257,769},{513,1},{769... | collective-permute-start | bytes 1277960 | tf_op jit(solution)/shard_map/ppermute | solution.py:23
  81.1 2.9 %collective-permute-start.8 = (bf16[416,512]{1,0:T(8,128)(2,1)S(1)}, bf16[416,512]{1,0:T(8,128)(2,1)S(1)}, u32[]{:S(2)}, u32[]{:S(2)}) collective-permute-start(bf16[416,512]{1,0:T(8,128)(2,1)S(1)} %late.1.refs_0_), channel_id=1, source_target_pairs={{0,256},{256,512},{512,768},{768,0},{1,257},{257,513},{513,769},{7... | collective-permute-start | bytes 1277960 | tf_op jit(solution)/shard_map/ppermute | solution.py:23
  84.0 4.8 %collective-permute-done.10.refs_3_ = bf16[416,512]{1,0:T(8,128)(2,1)S(1)} collective-permute-done((bf16[416,512]{1,0:T(8,128)(2,1)S(1)}, bf16[416,512]{1,0:T(8,128)(2,1)S(1)}, u32[]{:S(2)}, u32[]{:S(2)}) %collective-permute-start.10) | collective-permute-done | bytes 426016 | tf_op jit(solution)/shard_map/ppermute | solution.py:23
  88.8 1.4 %collective-permute-done.9.refs_2_ = bf16[416,512]{1,0:T(8,128)(2,1)S(1)} collective-permute-done((bf16[416,512]{1,0:T(8,128)(2,1)S(1)}, bf16[416,512]{1,0:T(8,128)(2,1)S(1)}, u32[]{:S(2)}, u32[]{:S(2)}) %collective-permute-start.9) | collective-permute-done | bytes 426016 | tf_op jit(solution)/shard_map/ppermute | solution.py:23
  90.2 4.5 %collective-permute-done.8.refs_1_ = bf16[416,512]{1,0:T(8,128)(2,1)S(1)} collective-permute-done((bf16[416,512]{1,0:T(8,128)(2,1)S(1)}, bf16[416,512]{1,0:T(8,128)(2,1)S(1)}, u32[]{:S(2)}, u32[]{:S(2)}) %collective-permute-start.8) | collective-permute-done | bytes 426016 | tf_op jit(solution)/shard_map/ppermute | solution.py:23
  94.7 1.8 %merge.1 = bf16[384,512]{1,0:T(8,128)(2,1)} custom-call(bf16[416,512]{1,0:T(8,128)(2,1)S(1)} %late.1.refs_0_, bf16[416,512]{1,0:T(8,128)(2,1)S(1)} %collective-permute-done.8.refs_1_, bf16[416,512]{1,0:T(8,128)(2,1)S(1)} %collective-permute-done.9.refs_2_, bf16[416,512]{1,0:T(8,128)(2,1)S(1)} %collective-permute-done.10.refs_3_), custom_call_target="tpu_custom_call" | custom-call | tf_op jit(solution)/shard_map/merge/pallas_call | solution.py:200
  (13 shorter events, 0.1 us)
Async XLA Ops:
  0.0 25.6 %collective-permute-start.3 = (bf16[96,256]{1,0:T(8,128)(2,1)}, bf16[96,256]{1,0:T(8,128)(2,1)S(1)}, u32[]{:S(2)}, u32[]{:S(2)}) collective-permute-start(bf16[96,256]{1,0:T(8,128)(2,1)} %bitcast.3), channel_id=1, source_target_pairs={{0,8},{1,9},{2,10},{3,11},{4,12},{5,13},{6,14},{7,15},{8,16},{9,17... | collective-permute-start | bytes 147464 | tf_op jit(solution)/shard_map/ppermute | solution.py:23
  15.7 18.2 %collective-permute-start = (bf16[96,256]{1,0:T(8,128)(2,1)}, bf16[96,256]{1,0:T(8,128)(2,1)S(1)}, u32[]{:S(2)}, u32[]{:S(2)}) collective-permute-start(bf16[96,256]{1,0:T(8,128)(2,1)} %bitcast.4), channel_id=1, source_target_pairs={{0,4},{1,5},{2,6},{3,7},{4,8},{5,9},{6,10},{7,11},{8,12},{9,13},{1... | collective-permute-start | bytes 147464 | tf_op jit(solution)/shard_map/ppermute | solution.py:23
  25.6 17.7 %collective-permute-start.4 = (bf16[96,256]{1,0:T(8,128)(2,1)S(1)}, bf16[96,256]{1,0:T(8,128)(2,1)S(1)}, u32[]{:S(2)}, u32[]{:S(2)}) collective-permute-start(bf16[96,256]{1,0:T(8,128)(2,1)S(1)} %collective-permute-done.3.refs_4_), channel_id=1, source_target_pairs={{0,4},{1,5},{2,6},{3,7},{4,8},{5,9},{6,10},{7,11},{8,12},{9,13},{1... | collective-permute-start | bytes 147464 | tf_op jit(solution)/shard_map/ppermute | solution.py:23
  34.8 15.9 %copy-start.1 = (bf16[1,1,96,1,256]{4,2,3,1,0:T(8,128)(2,1)S(1)}, bf16[1,1,96,1,256]{4,2,3,1,0:T(8,128)(2,1)}, u32[]{:S(2)}) copy-start(bf16[1,1,96,1,256]{4,2,3,1,0:T(8,128)(2,1)} %param.4) | copy-start | bytes 147460
  34.8 15.9 %collective-permute-start.1 = (bf16[192,256]{1,0:T(8,128)(2,1)S(1)}, bf16[192,256]{1,0:T(8,128)(2,1)S(1)}, u32[]{:S(2)}, u32[]{:S(2)}) collective-permute-start(bf16[192,256]{1,0:T(8,128)(2,1)S(1)} %pad_maximum_fusion.2), channel_id=1, source_target_pairs={{0,2},{1,3},{2,4},{3,5},{4,6},{5,7},{6,8},{7,9},{8,10},{9,11},{10,... | collective-permute-start | bytes 294920 | tf_op jit(solution)/shard_map/ppermute | solution.py:23
  43.3 20.8 %copy-start = (bf16[384,512]{1,0:T(8,128)(2,1)S(1)}, bf16[384,512]{1,0:T(8,128)(2,1)}, u32[]{:S(2)}) copy-start(bf16[384,512]{1,0:T(8,128)(2,1)} %q_ref.3) | copy-start | bytes 1179652
  43.3 12.7 %collective-permute-start.5 = (bf16[192,256]{1,0:T(8,128)(2,1)S(1)}, bf16[192,256]{1,0:T(8,128)(2,1)S(1)}, u32[]{:S(2)}, u32[]{:S(2)}) collective-permute-start(bf16[192,256]{1,0:T(8,128)(2,1)S(1)} %pad_maximum_fusion.3), channel_id=1, source_target_pairs={{0,2},{1,3},{2,4},{3,5},{4,6},{5,7},{6,8},{7,9},{8,10},{9,11},{10,... | collective-permute-start | bytes 294920 | tf_op jit(solution)/shard_map/ppermute | solution.py:23
  50.7 13.5 %collective-permute-start.2 = (bf16[384,256]{1,0:T(8,128)(2,1)S(1)}, bf16[384,256]{1,0:T(8,128)(2,1)S(1)}, u32[]{:S(2)}, u32[]{:S(2)}) collective-permute-start(bf16[384,256]{1,0:T(8,128)(2,1)S(1)} %pad_maximum_fusion), channel_id=1, source_target_pairs={{0,1},{1,2},{2,3},{3,4},{4,5},{5,6},{6,7},{7,8},{8,9},{9,10},{10,1... | collective-permute-start | bytes 589832 | tf_op jit(solution)/shard_map/ppermute | solution.py:23
  56.0 14.3 %collective-permute-start.6 = (bf16[384,256]{1,0:T(8,128)(2,1)S(1)}, bf16[384,256]{1,0:T(8,128)(2,1)S(1)}, u32[]{:S(2)}, u32[]{:S(2)}) collective-permute-start(bf16[384,256]{1,0:T(8,128)(2,1)S(1)} %pad_maximum_fusion.1), channel_id=1, source_target_pairs={{0,1},{1,2},{2,3},{3,4},{4,5},{5,6},{6,7},{7,8},{8,9},{9,10},{10,1... | collective-permute-start | bytes 589832 | tf_op jit(solution)/shard_map/ppermute | solution.py:23
  61.5 0.7 copy-start.2
  62.2 8.1 %collective-permute-start.7 = (bf16[96,256]{1,0:T(8,128)(2,1)S(1)}, bf16[96,256]{1,0:T(8,128)(2,1)S(1)}, u32[]{:S(2)}, u32[]{:S(2)}) collective-permute-start(bf16[96,256]{1,0:T(8,128)(2,1)S(1)} %slice.4), channel_id=1, source_target_pairs={{0,2},{1,3},{2,4},{3,5},{4,6},{5,7},{6,8},{7,9},{8,10},{9,11},{10,... | collective-permute-start | bytes 147464 | tf_op jit(solution)/shard_map/ppermute | solution.py:23
  73.7 15.1 %collective-permute-start.10 = (bf16[416,512]{1,0:T(8,128)(2,1)S(1)}, bf16[416,512]{1,0:T(8,128)(2,1)S(1)}, u32[]{:S(2)}, u32[]{:S(2)}) collective-permute-start(bf16[416,512]{1,0:T(8,128)(2,1)S(1)} %late.1.refs_0_), channel_id=1, source_target_pairs={{0,768},{256,0},{512,256},{768,512},{1,769},{257,1},{513,257},{769... | collective-permute-start | bytes 1277960 | tf_op jit(solution)/shard_map/ppermute | solution.py:23
  78.6 11.6 %collective-permute-start.9 = (bf16[416,512]{1,0:T(8,128)(2,1)S(1)}, bf16[416,512]{1,0:T(8,128)(2,1)S(1)}, u32[]{:S(2)}, u32[]{:S(2)}) collective-permute-start(bf16[416,512]{1,0:T(8,128)(2,1)S(1)} %late.1.refs_0_), channel_id=1, source_target_pairs={{0,512},{256,768},{512,0},{768,256},{1,513},{257,769},{513,1},{769... | collective-permute-start | bytes 1277960 | tf_op jit(solution)/shard_map/ppermute | solution.py:23
  81.1 13.5 %collective-permute-start.8 = (bf16[416,512]{1,0:T(8,128)(2,1)S(1)}, bf16[416,512]{1,0:T(8,128)(2,1)S(1)}, u32[]{:S(2)}, u32[]{:S(2)}) collective-permute-start(bf16[416,512]{1,0:T(8,128)(2,1)S(1)} %late.1.refs_0_), channel_id=1, source_target_pairs={{0,256},{256,512},{512,768},{768,0},{1,257},{257,513},{513,769},{7... | collective-permute-start | bytes 1277960 | tf_op jit(solution)/shard_map/ppermute | solution.py:23

commit v2 on v1

v2 whole, which is shorter than its diff:
```python
import functools
import math

import jax
import jax.numpy as jnp
from jax import lax
from jax.experimental import pallas as pl
from jax.experimental.pallas import tpu as pltpu
from jax.sharding import PartitionSpec as P

LOW = -1e30
FLOOR = -5e29
LANES = 128
NDOCS = 8
STAT_ROWS = 16
WHOLE = pl.BlockSpec(memory_space=pltpu.VMEM)
SCALARS = pl.BlockSpec(memory_space=pltpu.SMEM)
PLAN = (
    (6, (0,)),
    (6, (6,)),
    (3, (0, 6, 12)),
    (1, (0, 6, 12, 3, 9, 15)),
    (-1, (6, 12, 3, 9, 15)),
)
STAGES = ((-1, 0, 1, 2), (3,), (4,))


def distances_of(arrival):
    by, carried = PLAN[arrival]
    return (0,) if arrival < 0 else tuple(d + by for d in carried)


def shift(value, axis, by, count):
    return lax.ppermute(value, axis, [(i, (i + by) % count) for i in range(count)])


def joined(pieces, key_rows):
    runs = []
    for array, row in pieces:
        if runs and runs[-1][0] is array and runs[-1][2] == row:
            runs[-1][2] = row + key_rows
        else:
            runs.append([array, row, row + key_rows])
    cuts = [array if hi - lo == array.shape[0] else array[lo:hi] for array, lo, hi in runs]
    return jnp.concatenate(cuts) if len(cuts) > 1 else cuts[0]


def query_bounds(lengths, rows):
    place = lax.axis_index("tok") * rows + lax.broadcasted_iota(jnp.int32, (rows, LANES), 0)
    begin = jnp.zeros((rows, LANES), jnp.int32)
    end = jnp.int32(0)
    for i in range(NDOCS):
        end = end + lengths[i]
        begin = jnp.where(end <= place, end, begin)
    return place[:, :1], begin[:, :1]


def key_places(rows, key_rows, distances):
    tile, split = lax.axis_index("tok"), lax.axis_index("section")
    parts = []
    for d in distances:
        base = (tile - d) * rows + split * key_rows
        parts.append(base + lax.broadcasted_iota(jnp.int32, (1, key_rows), 1))
    return jnp.concatenate(parts, axis=1)


def scores_of(query, keys):
    return lax.dot_general(
        query, keys, (((1,), (1,)), ((), ())), preferred_element_type=jnp.float32
    )


def attend(factor, query, keys, values, visible, peak, total, sums):
    scores = jnp.where(visible, scores_of(query, keys), LOW)
    top = jnp.maximum(peak, jnp.max(scores, axis=1, keepdims=True))
    weights = jnp.exp2((scores - top) * factor).astype(jnp.bfloat16)
    mixed = jnp.dot(weights, values, preferred_element_type=jnp.float32)
    decay = jnp.exp2((peak - top) * factor)
    size = sums.shape[1]
    return top, total * decay + mixed[:, size : size + 1], sums * decay + mixed[:, :size]


def gathered(refs, size):
    keys = jnp.concatenate([ref[:, :size] for ref in refs], axis=0)
    values = jnp.concatenate([ref[:, size:] for ref in refs], axis=0)
    ones = jnp.ones((values.shape[0], LANES), values.dtype)
    return keys, jnp.concatenate([values, ones], axis=1)


def stage_kernel(factor, size, key_rows, stage, lengths, q_ref, *refs):
    first, last = stage == 0, stage == len(STAGES) - 1
    arrivals = STAGES[stage]
    rows, width = q_ref.shape
    heads = width // size
    place, begin = query_bounds(lengths, rows)
    if not first:
        sums_in, stats_in, *refs = refs
    if last:
        *kv_refs, out_ref = refs
    else:
        *kv_refs, sums_out, stats_out = refs
    if first:
        own_keys, own_values = gathered(kv_refs[:1], size)
        own_place = key_places(rows, key_rows, (0,))
        own_visible = (own_place <= place) & (own_place >= begin)
        arrivals, kv_refs = arrivals[1:], kv_refs[1:]
    keys, values = gathered(kv_refs, size)
    distances = [d for arrival in arrivals for d in distances_of(arrival)]
    visible = key_places(rows, key_rows, distances) >= begin
    lane = lax.broadcasted_iota(jnp.int32, (rows, LANES), 1)
    stats = jnp.full((rows, LANES), LOW, jnp.float32)
    for h in range(heads):
        cols = slice(h * size, (h + 1) * size)
        query = q_ref[:, cols]
        if first:
            state = (
                jnp.full((rows, 1), FLOOR, jnp.float32),
                jnp.zeros((rows, 1), jnp.float32),
                jnp.zeros((rows, size), jnp.float32),
            )
            state = attend(factor, query, own_keys, own_values, own_visible, *state)
        else:
            state = (stats_in[:, h : h + 1], stats_in[:, 4 + h : 5 + h], sums_in[:, cols])
        peak, total, sums = attend(factor, query, keys, values, visible, *state)
        if not last:
            stats = jnp.where(lane == h, peak, stats)
            stats = jnp.where(lane == 4 + h, total, stats)
            sums_out[:, cols] = sums
            continue
        some = total > 0.0
        level = jnp.where(some, peak * factor + jnp.log2(jnp.where(some, total, 1.0)), LOW)
        stats = jnp.where(lane == h, level, stats)
        share = jnp.where(some, 1.0 / jnp.where(some, total, 1.0), 0.0)
        out_ref[:rows, cols] = (sums * share).astype(jnp.bfloat16)
    if not last:
        stats_out[...] = stats
        return
    levels = jnp.transpose(stats)[:8]
    high = levels.astype(jnp.bfloat16).astype(jnp.float32)
    rest = levels - high
    middle = rest.astype(jnp.bfloat16).astype(jnp.float32)
    low = rest - middle
    row = lax.broadcasted_iota(jnp.int32, high.shape, 0)
    packed = jnp.concatenate([jnp.where(row < 4, high, pltpu.roll(middle, 4, 0)), low], axis=0)
    spare = jnp.zeros((STAT_ROWS, width - rows), jnp.float32)
    out_ref[rows:, :] = jnp.concatenate([packed, spare], axis=1).astype(jnp.bfloat16)


def merge_kernel(size, *refs):
    *parts, out_ref = refs
    rows = out_ref.shape[0]
    heads = out_ref.shape[1] // size
    levels = []
    for part in parts:
        packed = part[rows:, :].astype(jnp.float32)[:, :rows]
        levels.append((packed[:8] + pltpu.roll(packed[:8], 4, 0)) + packed[8:])
    top = functools.reduce(jnp.maximum, levels)
    terms = [jnp.exp2(level - top) for level in levels]
    total = (terms[0] + terms[2]) + (terms[1] + terms[3])
    shares = [term / total for term in terms]
    blank = jnp.zeros((LANES - 8 * len(parts), rows), jnp.float32)
    shares = jnp.transpose(jnp.concatenate(shares + [blank], axis=0))
    for h in range(heads):
        cols = slice(h * size, (h + 1) * size)
        terms = [
            part[:rows, cols].astype(jnp.float32) * shares[:, 8 * i + h : 8 * i + h + 1]
            for i, part in enumerate(parts)
        ]
        out_ref[:, cols] = ((terms[0] + terms[2]) + (terms[1] + terms[3])).astype(jnp.bfloat16)


def params():
    return pltpu.CompilerParams(vmem_limit_bytes=40 * 1024 * 1024)


def cost(rows, heads, keys, size):
    pairs = rows * heads * keys
    return pl.CostEstimate(
        flops=4 * pairs * size, bytes_accessed=2 * rows * heads * size, transcendentals=pairs
    )


def stage_call(factor, size, key_rows, stage, lengths, queries, state, chunks):
    rows, width = queries.shape
    keys = sum(len(distances_of(arrival)) for arrival in STAGES[stage]) * key_rows
    if stage == len(STAGES) - 1:
        out_shape = jax.ShapeDtypeStruct((rows + STAT_ROWS, width), jnp.bfloat16)
        out_specs = WHOLE
    else:
        out_shape = (
            jax.ShapeDtypeStruct((rows, width), jnp.float32),
            jax.ShapeDtypeStruct((rows, LANES), jnp.float32),
        )
        out_specs = (WHOLE, WHOLE)
    return pl.pallas_call(
        functools.partial(stage_kernel, factor, size, key_rows, stage),
        out_shape=out_shape,
        in_specs=[SCALARS] + [WHOLE] * (1 + len(state) + len(chunks)),
        out_specs=out_specs,
        compiler_params=params(),
        cost_estimate=cost(rows, width // size, keys, size),
        name="attend" + str(stage),
    )(lengths, queries, *state, *chunks)


def merge_call(size, rows, parts):
    width = parts[0].shape[1]
    return pl.pallas_call(
        functools.partial(merge_kernel, size),
        out_shape=jax.ShapeDtypeStruct((rows, width), jnp.bfloat16),
        in_specs=[WHOLE] * len(parts),
        out_specs=WHOLE,
        compiler_params=params(),
        name="merge",
    )(*parts)


def shards(tiles, splits, queries, key_values, lengths):
    rows = queries.shape[0]
    key_rows = key_values.shape[2]
    size = key_values.shape[4] // 2
    factor = size ** (-0.5) * math.log2(math.e)
    own = key_values.reshape(key_rows, 2 * size)
    held = {0: (own, 0)}
    arrived = []
    for by, carried in PLAN:
        cargo = joined([held[d] for d in carried], key_rows)
        result = shift(cargo, "tok", by, tiles)
        arrived.append(result)
        for i, d in enumerate(carried):
            held[d] = (cargo, i * key_rows)
            held[d + by] = (result, i * key_rows)
    state = ()
    for stage, arrivals in enumerate(STAGES):
        chunks = [own if arrival < 0 else arrived[arrival] for arrival in arrivals]
        state = stage_call(factor, size, key_rows, stage, lengths, queries, state, chunks)
    part = state
    parts = [part] + [shift(part, "section", by, splits) for by in range(1, splits)]
    return merge_call(size, rows, parts)


def solution(mesh):
    return jax.shard_map(
        functools.partial(shards, mesh.shape["tok"], mesh.shape["section"]),
        mesh=mesh,
        in_specs=(P("tok", "head"), P("tok", "section", None, "head", None), P()),
        out_specs=P("tok", "head"),
        check_vma=False,
    )
```

time: 97.3 us -> 99.5 us (1.023)
  starting transfers between devices: 70.1 us -> 40.2 us
  waiting for transfers between devices: 15.6 us -> 44.9 us
  Pallas kernels: 9.08 us -> 13 us
    ppermute x11 -> x8, starting transfers between devices: 70.1 us -> 40.2 us  [shift(): lax.ppermute(value, axis, [(i, (i + by) % count) for i in range(count)])]
    ppermute x11 -> x8, waiting for transfers between devices: 15.6 us -> 44.9 us  [shift(): lax.ppermute(value, axis, [(i, (i + by) % count) for i in range(count)])]
    pallas_call x3 -> x4, Pallas kernels: 9.08 us -> 13 us  [the longest x3 11.1 us: stage_call(): pl.pallas_call(functools.partial(stage_kernel, factor, size, key_rows, st...]
  transfers between devices with their start and end apart: 11 -> 8, of which waited for: 7 -> 6; matrix products, arithmetic and copies ran while one was open for 1% -> 0% of each run, Pallas kernels for 4% -> 7%
where the time goes in v2:
time: 99.5 us; the launch traced here: 99.1 us
  waiting for transfers between devices  44.9 us (45%)
  starting transfers between devices  40.2 us (40%)
  Pallas kernels  13 us (13%)
    ppermute x8, waiting for transfers between devices, shift(): lax.ppermute(value, axis, [(i, (i + by) % count) for i in range(count)])  44.9 us
    ppermute x8, starting transfers between devices, shift(): lax.ppermute(value, axis, [(i, (i + by) % count) for i in range(count)])  40.2 us
    pallas_call x3, Pallas kernels, stage_call(): pl.pallas_call(functools.partial(stage_kernel, factor, size, key_rows, st...  11.1 us
  transfers between devices with their start and end apart: 8, of which 6 were waited for; matrix products, arithmetic and copies ran while one was open for 0% of the time, Pallas kernels for 7%

profile of v2, /device:TPU:6, one launch (start us, length us, event | category | flops | bytes accessed | tf_op | source)
XLA Modules:
  0.0 99.1 jit_solution(10689389918324287230)
XLA Ops:
  0.0 11.9 %collective-permute-start = (bf16[96,256]{1,0:T(8,128)(2,1)}, bf16[96,256]{1,0:T(8,128)(2,1)S(1)}, u32[]{:S(2)}, u32[]{:S(2)}) collective-permute-start(bf16[96,256]{1,0:T(8,128)(2,1)} %bitcast.1), channel_id=1, source_target_pairs={{0,6},{1,7},{2,8},{3,9},{4,10},{5,11},{6,12},{7,13},{8,14},{9,15},... | collective-permute-start | bytes 147464 | tf_op jit(solution)/shard_map/ppermute | solution.py:34
  11.9 12.7 %collective-permute-done.refs_1_ = bf16[96,256]{1,0:T(8,128)(2,1)S(1)} collective-permute-done((bf16[96,256]{1,0:T(8,128)(2,1)}, bf16[96,256]{1,0:T(8,128)(2,1)S(1)}, u32[]{:S(2)}, u32[]{:S(2)}) %collective-permute-start) | collective-permute-done | bytes 49184 | tf_op jit(solution)/shard_map/ppermute | solution.py:34
  24.6 4.2 %collective-permute-start.1 = (bf16[96,256]{1,0:T(8,128)(2,1)S(1)}, bf16[96,256]{1,0:T(8,128)(2,1)S(1)}, u32[]{:S(2)}, u32[]{:S(2)}) collective-permute-start(bf16[96,256]{1,0:T(8,128)(2,1)S(1)} %collective-permute-done.refs_1_), channel_id=1, source_target_pairs={{0,6},{1,7},{2,8},{3,9},{4,10},{5,11},{6,12},{7,13},{8,14},{9,15},... | collective-permute-start | bytes 147464 | tf_op jit(solution)/shard_map/ppermute | solution.py:34
  28.8 10.0 %collective-permute-done.1.refs_2_ = bf16[96,256]{1,0:T(8,128)(2,1)S(1)} collective-permute-done((bf16[96,256]{1,0:T(8,128)(2,1)S(1)}, bf16[96,256]{1,0:T(8,128)(2,1)S(1)}, u32[]{:S(2)}, u32[]{:S(2)}) %collective-permute-start.1) | collective-permute-done | bytes 49184 | tf_op jit(solution)/shard_map/ppermute | solution.py:34
  38.8 0.8 pad_maximum_fusion.2
  39.6 0.0 copy-start
  39.6 6.7 %collective-permute-start.2 = (bf16[288,256]{1,0:T(8,128)(2,1)S(1)}, bf16[288,256]{1,0:T(8,128)(2,1)S(1)}, u32[]{:S(2)}, u32[]{:S(2)}) collective-permute-start(bf16[288,256]{1,0:T(8,128)(2,1)S(1)} %pad_maximum_fusion.2), channel_id=1, source_target_pairs={{0,3},{1,4},{2,5},{3,6},{4,7},{5,8},{6,9},{7,10},{8,11},{9,12},{10... | collective-permute-start | bytes 442376 | tf_op jit(solution)/shard_map/ppermute | solution.py:34
  46.4 10.4 %collective-permute-done.2.refs_3_ = bf16[288,256]{1,0:T(8,128)(2,1)S(1)} collective-permute-done((bf16[288,256]{1,0:T(8,128)(2,1)S(1)}, bf16[288,256]{1,0:T(8,128)(2,1)S(1)}, u32[]{:S(2)}, u32[]{:S(2)}) %collective-permute-start.2) | collective-permute-done | bytes 147488 | tf_op jit(solution)/shard_map/ppermute | solution.py:34
  56.8 0.0 copy-done.1
  56.8 0.0 copy-start.2
  56.8 1.9 %collective-permute-start.3 = (bf16[576,256]{1,0:T(8,128)(2,1)S(1)}, bf16[576,256]{1,0:T(8,128)(2,1)S(1)}, u32[]{:S(2)}, u32[]{:S(2)}) collective-permute-start(bf16[576,256]{1,0:T(8,128)(2,1)S(1)} %pad_maximum_fusion), channel_id=1, source_target_pairs={{0,1},{1,2},{2,3},{3,4},{4,5},{5,6},{6,7},{7,8},{8,9},{9,10},{10,1... | collective-permute-start | bytes 884744 | tf_op jit(solution)/shard_map/ppermute | solution.py:34
  58.8 5.1 %collective-permute-start.4 = (bf16[480,256]{1,0:T(8,128)(2,1)S(1)}, bf16[480,256]{1,0:T(8,128)(2,1)S(1)}, u32[]{:S(2)}, u32[]{:S(2)}) collective-permute-start(bf16[480,256]{1,0:T(8,128)(2,1)S(1)} %pad_maximum_fusion.1), channel_id=1, source_target_pairs={{0,31},{1,0},{2,1},{3,2},{4,3},{5,4},{6,5},{7,6},{8,7},{9,8},{10,9... | collective-permute-start | bytes 737288 | tf_op jit(solution)/shard_map/ppermute | solution.py:34
  64.0 2.7 %attend0.1 = (f32[384,512]{1,0:T(8,128)S(1)}, f32[384,128]{1,0:T(8,128)S(1)}) custom-call(s32[8]{0:T(128)S(1)} %copy-done.2, bf16[384,512]{1,0:T(8,128)(2,1)S(1)} %copy-done, bf16[96,256]{1,0:T(8,128)(2,1)S(1)} %bitcast.4, bf16[96,256]{1,0:T(8,128)(2,1)S(1)} %collective-permute-done.refs_1_, bf16[96,256]{1,0:T(8,128)(2,1)S(1)} %collective-permute-done.1.refs_2_, ...), custom_call_target="tpu_custom_call" | custom-call | flops 452984832 | bytes 393216 | tf_op jit(solution)/shard_map/attend0/pallas_call | solution.py:195
  66.7 0.0 collective-permute-done.3.refs_2_
  66.7 4.0 %attend1.1 = (f32[384,512]{1,0:T(8,128)S(1)}, f32[384,128]{1,0:T(8,128)S(1)}) custom-call(s32[8]{0:T(128)S(1)} %copy-done.2, bf16[384,512]{1,0:T(8,128)(2,1)S(1)} %copy-done, f32[384,512]{1,0:T(8,128)S(1)} %get-tuple-element.9.refs_0_, f32[384,128]{1,0:T(8,128)S(1)} %get-tuple-element.10.refs_1_, bf16[576,256]{1,0:T(8,128)(2,1)S(1)} %collective-permute-done.3.refs_2_), custom_call_target="tpu_custom_call" | custom-call | flops 452984832 | bytes 393216 | tf_op jit(solution)/shard_map/attend1/pallas_call | solution.py:195
  70.7 0.0 collective-permute-done.4.refs_2_
  70.7 4.4 %attend2.1.refs_0_ = bf16[400,512]{1,0:T(8,128)(2,1)S(1)} custom-call(s32[8]{0:T(128)S(1)} %copy-done.2, bf16[384,512]{1,0:T(8,128)(2,1)S(1)} %copy-done, f32[384,512]{1,0:T(8,128)S(1)} %get-tuple-element.11.refs_0_, f32[384,128]{1,0:T(8,128)S(1)} %get-tuple-element.12.refs_1_, bf16[480,256]{1,0:T(8,128)(2,1)S(1)} %collective-permute-done.4.refs_2_), custom_call_target="tpu_custom_call" | custom-call | flops 377487360 | bytes 393216 | tf_op jit(solution)/shard_map/attend2/pallas_call | solution.py:195
  75.1 4.9 %collective-permute-start.7 = (bf16[400,512]{1,0:T(8,128)(2,1)S(1)}, bf16[400,512]{1,0:T(8,128)(2,1)S(1)}, u32[]{:S(2)}, u32[]{:S(2)}) collective-permute-start(bf16[400,512]{1,0:T(8,128)(2,1)S(1)} %attend2.1.refs_0_), channel_id=1, source_target_pairs={{0,768},{256,0},{512,256},{768,512},{1,769},{257,1},{513,257},{769... | collective-permute-start | bytes 1228808 | tf_op jit(solution)/shard_map/ppermute | solution.py:34
  80.1 2.5 %collective-permute-start.6 = (bf16[400,512]{1,0:T(8,128)(2,1)S(1)}, bf16[400,512]{1,0:T(8,128)(2,1)S(1)}, u32[]{:S(2)}, u32[]{:S(2)}) collective-permute-start(bf16[400,512]{1,0:T(8,128)(2,1)S(1)} %attend2.1.refs_0_), channel_id=1, source_target_pairs={{0,512},{256,768},{512,0},{768,256},{1,513},{257,769},{513,1},{769... | collective-permute-start | bytes 1228808 | tf_op jit(solution)/shard_map/ppermute | solution.py:34
  82.6 2.9 %collective-permute-start.5 = (bf16[400,512]{1,0:T(8,128)(2,1)S(1)}, bf16[400,512]{1,0:T(8,128)(2,1)S(1)}, u32[]{:S(2)}, u32[]{:S(2)}) collective-permute-start(bf16[400,512]{1,0:T(8,128)(2,1)S(1)} %attend2.1.refs_0_), channel_id=1, source_target_pairs={{0,256},{256,512},{512,768},{768,0},{1,257},{257,513},{513,769},{7... | collective-permute-start | bytes 1228808 | tf_op jit(solution)/shard_map/ppermute | solution.py:34
  85.5 6.1 %collective-permute-done.7.refs_3_ = bf16[400,512]{1,0:T(8,128)(2,1)S(1)} collective-permute-done((bf16[400,512]{1,0:T(8,128)(2,1)S(1)}, bf16[400,512]{1,0:T(8,128)(2,1)S(1)}, u32[]{:S(2)}, u32[]{:S(2)}) %collective-permute-start.7) | collective-permute-done | bytes 409632 | tf_op jit(solution)/shard_map/ppermute | solution.py:34
  91.6 1.4 %collective-permute-done.6.refs_2_ = bf16[400,512]{1,0:T(8,128)(2,1)S(1)} collective-permute-done((bf16[400,512]{1,0:T(8,128)(2,1)S(1)}, bf16[400,512]{1,0:T(8,128)(2,1)S(1)}, u32[]{:S(2)}, u32[]{:S(2)}) %collective-permute-start.6) | collective-permute-done | bytes 409632 | tf_op jit(solution)/shard_map/ppermute | solution.py:34
  93.0 4.2 %collective-permute-done.5.refs_1_ = bf16[400,512]{1,0:T(8,128)(2,1)S(1)} collective-permute-done((bf16[400,512]{1,0:T(8,128)(2,1)S(1)}, bf16[400,512]{1,0:T(8,128)(2,1)S(1)}, u32[]{:S(2)}, u32[]{:S(2)}) %collective-permute-start.5) | collective-permute-done | bytes 409632 | tf_op jit(solution)/shard_map/ppermute | solution.py:34
  97.2 1.8 %merge.1 = bf16[384,512]{1,0:T(8,128)(2,1)} custom-call(bf16[400,512]{1,0:T(8,128)(2,1)S(1)} %attend2.1.refs_0_, bf16[400,512]{1,0:T(8,128)(2,1)S(1)} %collective-permute-done.5.refs_1_, bf16[400,512]{1,0:T(8,128)(2,1)S(1)} %collective-permute-done.6.refs_2_, bf16[400,512]{1,0:T(8,128)(2,1)S(1)} %collective-permute-done.7.refs_3_), custom_call_target="tpu_custom_call" | custom-call | tf_op jit(solution)/shard_map/merge/pallas_call | solution.py:208
  (5 shorter events, 0.0 us)
Async XLA Ops:
  0.0 56.8 %copy-start.1 = (bf16[1,1,96,1,256]{4,2,3,1,0:T(8,128)(2,1)S(1)}, bf16[1,1,96,1,256]{4,2,3,1,0:T(8,128)(2,1)}, u32[]{:S(2)}) copy-start(bf16[1,1,96,1,256]{4,2,3,1,0:T(8,128)(2,1)} %param.4) | copy-start | bytes 147460
  0.0 24.6 %collective-permute-start = (bf16[96,256]{1,0:T(8,128)(2,1)}, bf16[96,256]{1,0:T(8,128)(2,1)S(1)}, u32[]{:S(2)}, u32[]{:S(2)}) collective-permute-start(bf16[96,256]{1,0:T(8,128)(2,1)} %bitcast.1), channel_id=1, source_target_pairs={{0,6},{1,7},{2,8},{3,9},{4,10},{5,11},{6,12},{7,13},{8,14},{9,15},... | collective-permute-start | bytes 147464 | tf_op jit(solution)/shard_map/ppermute | solution.py:34
  24.6 14.2 %collective-permute-start.1 = (bf16[96,256]{1,0:T(8,128)(2,1)S(1)}, bf16[96,256]{1,0:T(8,128)(2,1)S(1)}, u32[]{:S(2)}, u32[]{:S(2)}) collective-permute-start(bf16[96,256]{1,0:T(8,128)(2,1)S(1)} %collective-permute-done.refs_1_), channel_id=1, source_target_pairs={{0,6},{1,7},{2,8},{3,9},{4,10},{5,11},{6,12},{7,13},{8,14},{9,15},... | collective-permute-start | bytes 147464 | tf_op jit(solution)/shard_map/ppermute | solution.py:34
  39.6 24.3 %copy-start = (bf16[384,512]{1,0:T(8,128)(2,1)S(1)}, bf16[384,512]{1,0:T(8,128)(2,1)}, u32[]{:S(2)}) copy-start(bf16[384,512]{1,0:T(8,128)(2,1)} %q_ref.5) | copy-start | bytes 1179652
  39.6 17.2 %collective-permute-start.2 = (bf16[288,256]{1,0:T(8,128)(2,1)S(1)}, bf16[288,256]{1,0:T(8,128)(2,1)S(1)}, u32[]{:S(2)}, u32[]{:S(2)}) collective-permute-start(bf16[288,256]{1,0:T(8,128)(2,1)S(1)} %pad_maximum_fusion.2), channel_id=1, source_target_pairs={{0,3},{1,4},{2,5},{3,6},{4,7},{5,8},{6,9},{7,10},{8,11},{9,12},{10... | collective-permute-start | bytes 442376 | tf_op jit(solution)/shard_map/ppermute | solution.py:34
  56.8 7.1 %copy-start.2 = (s32[8]{0:T(128)S(1)}, s32[8]{0:T(128)}, u32[]{:S(2)}) copy-start(s32[8]{0:T(128)} %lengths.5) | copy-start | bytes 100
  56.8 9.9 %collective-permute-start.3 = (bf16[576,256]{1,0:T(8,128)(2,1)S(1)}, bf16[576,256]{1,0:T(8,128)(2,1)S(1)}, u32[]{:S(2)}, u32[]{:S(2)}) collective-permute-start(bf16[576,256]{1,0:T(8,128)(2,1)S(1)} %pad_maximum_fusion), channel_id=1, source_target_pairs={{0,1},{1,2},{2,3},{3,4},{4,5},{5,6},{6,7},{7,8},{8,9},{9,10},{10,1... | collective-permute-start | bytes 884744 | tf_op jit(solution)/shard_map/ppermute | solution.py:34
  58.8 11.9 %collective-permute-start.4 = (bf16[480,256]{1,0:T(8,128)(2,1)S(1)}, bf16[480,256]{1,0:T(8,128)(2,1)S(1)}, u32[]{:S(2)}, u32[]{:S(2)}) collective-permute-start(bf16[480,256]{1,0:T(8,128)(2,1)S(1)} %pad_maximum_fusion.1), channel_id=1, source_target_pairs={{0,31},{1,0},{2,1},{3,2},{4,3},{5,4},{6,5},{7,6},{8,7},{9,8},{10,9... | collective-permute-start | bytes 737288 | tf_op jit(solution)/shard_map/ppermute | solution.py:34
  75.1 16.5 %collective-permute-start.7 = (bf16[400,512]{1,0:T(8,128)(2,1)S(1)}, bf16[400,512]{1,0:T(8,128)(2,1)S(1)}, u32[]{:S(2)}, u32[]{:S(2)}) collective-permute-start(bf16[400,512]{1,0:T(8,128)(2,1)S(1)} %attend2.1.refs_0_), channel_id=1, source_target_pairs={{0,768},{256,0},{512,256},{768,512},{1,769},{257,1},{513,257},{769... | collective-permute-start | bytes 1228808 | tf_op jit(solution)/shard_map/ppermute | solution.py:34
  80.1 12.9 %collective-permute-start.6 = (bf16[400,512]{1,0:T(8,128)(2,1)S(1)}, bf16[400,512]{1,0:T(8,128)(2,1)S(1)}, u32[]{:S(2)}, u32[]{:S(2)}) collective-permute-start(bf16[400,512]{1,0:T(8,128)(2,1)S(1)} %attend2.1.refs_0_), channel_id=1, source_target_pairs={{0,512},{256,768},{512,0},{768,256},{1,513},{257,769},{513,1},{769... | collective-permute-start | bytes 1228808 | tf_op jit(solution)/shard_map/ppermute | solution.py:34
  82.6 14.6 %collective-permute-start.5 = (bf16[400,512]{1,0:T(8,128)(2,1)S(1)}, bf16[400,512]{1,0:T(8,128)(2,1)S(1)}, u32[]{:S(2)}, u32[]{:S(2)}) collective-permute-start(bf16[400,512]{1,0:T(8,128)(2,1)S(1)} %attend2.1.refs_0_), channel_id=1, source_target_pairs={{0,256},{256,512},{512,768},{768,0},{1,257},{257,513},{513,769},{7... | collective-permute-start | bytes 1228808 | tf_op jit(solution)/shard_map/ppermute | solution.py:34

commit v3 on v2

--- a/solution.py
+++ b/solution.py
@@ -52,7 +52,22 @@
     for i in range(NDOCS):
         end = end + lengths[i]
         begin = jnp.where(end <= place, end, begin)
-    return place[:, :1], begin[:, :1]
+    return begin
+
+
+def bounds_kernel(lengths, begin_ref):
+    begin_ref[...] = query_bounds(lengths, begin_ref.shape[0])
+
+
+def bounds_call(lengths, rows):
+    return pl.pallas_call(
+        bounds_kernel,
+        out_shape=jax.ShapeDtypeStruct((rows, LANES), jnp.int32),
+        in_specs=[SCALARS],
+        out_specs=WHOLE,
+        compiler_params=params(),
+        name="bounds",
+    )(lengths)
 
 
 def key_places(rows, key_rows, distances):
@@ -77,7 +92,7 @@
     mixed = jnp.dot(weights, values, preferred_element_type=jnp.float32)
     decay = jnp.exp2((peak - top) * factor)
     size = sums.shape[1]
-    return top, total * decay + mixed[:, size : size + 1], sums * decay + mixed[:, :size]
+    return top, total * decay + mixed[:, size:], sums * decay + mixed[:, :size]
 
 
 def gathered(refs, size):
@@ -87,19 +102,20 @@
     return keys, jnp.concatenate([values, ones], axis=1)
 
 
-def stage_kernel(factor, size, key_rows, stage, lengths, q_ref, *refs):
+def stage_kernel(factor, size, key_rows, stage, begin_ref, q_ref, *refs):
     first, last = stage == 0, stage == len(STAGES) - 1
     arrivals = STAGES[stage]
     rows, width = q_ref.shape
     heads = width // size
-    place, begin = query_bounds(lengths, rows)
+    begin = begin_ref[:, :1]
     if not first:
-        sums_in, stats_in, *refs = refs
+        sums_in, totals_in, stats_in, *refs = refs
     if last:
         *kv_refs, out_ref = refs
     else:
-        *kv_refs, sums_out, stats_out = refs
+        *kv_refs, sums_out, totals_out, stats_out = refs
     if first:
+        place = lax.axis_index("tok") * rows + lax.broadcasted_iota(jnp.int32, (rows, 1), 0)
         own_keys, own_values = gathered(kv_refs[:1], size)
         own_place = key_places(rows, key_rows, (0,))
         own_visible = (own_place <= place) & (own_place >= begin)
@@ -109,32 +125,33 @@
     visible = key_places(rows, key_rows, distances) >= begin
     lane = lax.broadcasted_iota(jnp.int32, (rows, LANES), 1)
     stats = jnp.full((rows, LANES), LOW, jnp.float32)
+    packed = jnp.ones((rows, LANES), jnp.float32)
     for h in range(heads):
         cols = slice(h * size, (h + 1) * size)
         query = q_ref[:, cols]
         if first:
             state = (
                 jnp.full((rows, 1), FLOOR, jnp.float32),
-                jnp.zeros((rows, 1), jnp.float32),
+                jnp.zeros((rows, LANES), jnp.float32),
                 jnp.zeros((rows, size), jnp.float32),
             )
             state = attend(factor, query, own_keys, own_values, own_visible, *state)
         else:
-            state = (stats_in[:, h : h + 1], stats_in[:, 4 + h : 5 + h], sums_in[:, cols])
+            state = (stats_in[:, h : h + 1], totals_in[:, cols], sums_in[:, cols])
         peak, total, sums = attend(factor, query, keys, values, visible, *state)
         if not last:
             stats = jnp.where(lane == h, peak, stats)
-            stats = jnp.where(lane == 4 + h, total, stats)
+            totals_out[:, cols] = total
             sums_out[:, cols] = sums
             continue
-        some = total > 0.0
-        level = jnp.where(some, peak * factor + jnp.log2(jnp.where(some, total, 1.0)), LOW)
-        stats = jnp.where(lane == h, level, stats)
-        share = jnp.where(some, 1.0 / jnp.where(some, total, 1.0), 0.0)
-        out_ref[:rows, cols] = (sums * share).astype(jnp.bfloat16)
+        stats = jnp.where(lane == h, peak, stats)
+        packed = jnp.where(lane == h, total, packed)
+        out_ref[:rows, cols] = (sums / jnp.maximum(total, 1e-30)).astype(jnp.bfloat16)
     if not last:
         stats_out[...] = stats
         return
+    stats = stats * factor + jnp.log2(jnp.maximum(packed, 1e-30))
+    stats = jnp.where(packed > 0.0, stats, LOW)
     levels = jnp.transpose(stats)[:8]
     high = levels.astype(jnp.bfloat16).astype(jnp.float32)
     rest = levels - high
@@ -180,7 +197,7 @@
     )
 
 
-def stage_call(factor, size, key_rows, stage, lengths, queries, state, chunks):
+def stage_call(factor, size, key_rows, stage, begin, queries, state, chunks):
     rows, width = queries.shape
     keys = sum(len(distances_of(arrival)) for arrival in STAGES[stage]) * key_rows
     if stage == len(STAGES) - 1:
@@ -189,18 +206,19 @@
     else:
         out_shape = (
             jax.ShapeDtypeStruct((rows, width), jnp.float32),
+            jax.ShapeDtypeStruct((rows, width), jnp.float32),
             jax.ShapeDtypeStruct((rows, LANES), jnp.float32),
         )
-        out_specs = (WHOLE, WHOLE)
+        out_specs = (WHOLE, WHOLE, WHOLE)
     return pl.pallas_call(
         functools.partial(stage_kernel, factor, size, key_rows, stage),
         out_shape=out_shape,
-        in_specs=[SCALARS] + [WHOLE] * (1 + len(state) + len(chunks)),
+        in_specs=[WHOLE] * (2 + len(state) + len(chunks)),
         out_specs=out_specs,
         compiler_params=params(),
         cost_estimate=cost(rows, width // size, keys, size),
         name="attend" + str(stage),
-    )(lengths, queries, *state, *chunks)
+    )(begin, queries, *state, *chunks)
 
 
 def merge_call(size, rows, parts):
@@ -230,10 +248,11 @@
         for i, d in enumerate(carried):
             held[d] = (cargo, i * key_rows)
             held[d + by] = (result, i * key_rows)
+    begin = bounds_call(lengths, rows)
     state = ()
     for stage, arrivals in enumerate(STAGES):
         chunks = [own if arrival < 0 else arrived[arrival] for arrival in arrivals]
-        state = stage_call(factor, size, key_rows, stage, lengths, queries, state, chunks)
+        state = stage_call(factor, size, key_rows, stage, begin, queries, state, chunks)
     part = state
     parts = [part] + [shift(part, "section", by, splits) for by in range(1, splits)]
     return merge_call(size, rows, parts)

time: 99.5 us -> 95.8 us (0.963)
  Pallas kernels: 13 us -> 9.47 us
    pallas_call x3, Pallas kernels: 11.1 us -> 6.97 us  [stage_call(): pl.pallas_call(functools.partial(stage_kernel, factor, size, key_rows, st...]
  transfers between devices with their start and end apart: 8 -> 8, of which waited for: 6 -> 6; matrix products, arithmetic and copies ran while one was open for 0% -> 0% of each run, Pallas kernels for 7% -> 6%
where the time goes in v3:
time: 95.8 us; the launch traced here: 95.3 us
  waiting for transfers between devices  44.6 us (47%)
  starting transfers between devices  40.3 us (42%)
  Pallas kernels  9.47 us (10%)
    ppermute x8, waiting for transfers between devices, shift(): lax.ppermute(value, axis, [(i, (i + by) % count) for i in range(count)])  44.6 us
    ppermute x8, starting transfers between devices, shift(): lax.ppermute(value, axis, [(i, (i + by) % count) for i in range(count)])  40.3 us
    pallas_call x3, Pallas kernels, stage_call(): pl.pallas_call(functools.partial(stage_kernel, factor, size, key_rows, st...  6.97 us
  transfers between devices with their start and end apart: 8, of which 6 were waited for; matrix products, arithmetic and copies ran while one was open for 0% of the time, Pallas kernels for 6%

profile of v3, /device:TPU:6, one launch (start us, length us, event | category | flops | bytes accessed | tf_op | source)
XLA Modules:
  0.0 95.3 jit_solution(9533165236159028407)
XLA Ops:
  0.0 11.9 %collective-permute-start = (bf16[96,256]{1,0:T(8,128)(2,1)}, bf16[96,256]{1,0:T(8,128)(2,1)S(1)}, u32[]{:S(2)}, u32[]{:S(2)}) collective-permute-start(bf16[96,256]{1,0:T(8,128)(2,1)} %bitcast.1), channel_id=1, source_target_pairs={{0,6},{1,7},{2,8},{3,9},{4,10},{5,11},{6,12},{7,13},{8,14},{9,15},... | collective-permute-start | bytes 147464 | tf_op jit(solution)/shard_map/ppermute | solution.py:34
  11.9 12.7 %collective-permute-done.refs_1_ = bf16[96,256]{1,0:T(8,128)(2,1)S(1)} collective-permute-done((bf16[96,256]{1,0:T(8,128)(2,1)}, bf16[96,256]{1,0:T(8,128)(2,1)S(1)}, u32[]{:S(2)}, u32[]{:S(2)}) %collective-permute-start) | collective-permute-done | bytes 49184 | tf_op jit(solution)/shard_map/ppermute | solution.py:34
  24.6 4.2 %collective-permute-start.1 = (bf16[96,256]{1,0:T(8,128)(2,1)S(1)}, bf16[96,256]{1,0:T(8,128)(2,1)S(1)}, u32[]{:S(2)}, u32[]{:S(2)}) collective-permute-start(bf16[96,256]{1,0:T(8,128)(2,1)S(1)} %collective-permute-done.refs_1_), channel_id=1, source_target_pairs={{0,6},{1,7},{2,8},{3,9},{4,10},{5,11},{6,12},{7,13},{8,14},{9,15},... | collective-permute-start | bytes 147464 | tf_op jit(solution)/shard_map/ppermute | solution.py:34
  28.8 10.0 %collective-permute-done.1.refs_2_ = bf16[96,256]{1,0:T(8,128)(2,1)S(1)} collective-permute-done((bf16[96,256]{1,0:T(8,128)(2,1)S(1)}, bf16[96,256]{1,0:T(8,128)(2,1)S(1)}, u32[]{:S(2)}, u32[]{:S(2)}) %collective-permute-start.1) | collective-permute-done | bytes 49184 | tf_op jit(solution)/shard_map/ppermute | solution.py:34
  38.8 0.8 pad_maximum_fusion.2
  39.6 6.6 %collective-permute-start.2 = (bf16[288,256]{1,0:T(8,128)(2,1)S(1)}, bf16[288,256]{1,0:T(8,128)(2,1)S(1)}, u32[]{:S(2)}, u32[]{:S(2)}) collective-permute-start(bf16[288,256]{1,0:T(8,128)(2,1)S(1)} %pad_maximum_fusion.2), channel_id=1, source_target_pairs={{0,3},{1,4},{2,5},{3,6},{4,7},{5,8},{6,9},{7,10},{8,11},{9,12},{10... | collective-permute-start | bytes 442376 | tf_op jit(solution)/shard_map/ppermute | solution.py:34
  46.3 10.4 %collective-permute-done.2.refs_3_ = bf16[288,256]{1,0:T(8,128)(2,1)S(1)} collective-permute-done((bf16[288,256]{1,0:T(8,128)(2,1)S(1)}, bf16[288,256]{1,0:T(8,128)(2,1)S(1)}, u32[]{:S(2)}, u32[]{:S(2)}) %collective-permute-start.2) | collective-permute-done | bytes 147488 | tf_op jit(solution)/shard_map/ppermute | solution.py:34
  56.7 0.0 copy-start.2
  56.7 0.0 copy-start
  56.7 2.1 %collective-permute-start.3 = (bf16[576,256]{1,0:T(8,128)(2,1)S(1)}, bf16[576,256]{1,0:T(8,128)(2,1)S(1)}, u32[]{:S(2)}, u32[]{:S(2)}) collective-permute-start(bf16[576,256]{1,0:T(8,128)(2,1)S(1)} %pad_maximum_fusion), channel_id=1, source_target_pairs={{0,1},{1,2},{2,3},{3,4},{4,5},{5,6},{6,7},{7,8},{8,9},{9,10},{10,1... | collective-permute-start | bytes 884744 | tf_op jit(solution)/shard_map/ppermute | solution.py:34
  58.8 5.1 %collective-permute-start.4 = (bf16[480,256]{1,0:T(8,128)(2,1)S(1)}, bf16[480,256]{1,0:T(8,128)(2,1)S(1)}, u32[]{:S(2)}, u32[]{:S(2)}) collective-permute-start(bf16[480,256]{1,0:T(8,128)(2,1)S(1)} %pad_maximum_fusion.1), channel_id=1, source_target_pairs={{0,31},{1,0},{2,1},{3,2},{4,3},{5,4},{6,5},{7,6},{8,7},{9,8},{10,9... | collective-permute-start | bytes 737288 | tf_op jit(solution)/shard_map/ppermute | solution.py:34
  64.0 0.7 bounds.1.begin_ref
  64.7 2.2 %attend0.1 = (f32[384,512]{1,0:T(8,128)S(1)}, f32[384,512]{1,0:T(8,128)S(1)}, f32[384,128]{1,0:T(8,128)S(1)}) custom-call(s32[384,128]{1,0:T(8,128)S(1)} %bounds.1.begin_ref, bf16[384,512]{1,0:T(8,128)(2,1)S(1)} %copy-done, bf16[96,256]{1,0:T(8,128)(2,1)S(1)} %bitcast.4, bf16[96,256]{1,0:T(8,128)(2,1)S(1)} %collective-permute-done.refs_1_, ...), custom_call_target="tpu_custom_call" | custom-call | flops 452984832 | bytes 393216 | tf_op jit(solution)/shard_map/attend0/pallas_call | solution.py:213
  66.9 0.0 collective-permute-done.3.refs_3_
  66.9 2.7 %attend1.1 = (f32[384,512]{1,0:T(8,128)S(1)}, f32[384,512]{1,0:T(8,128)S(1)}, f32[384,128]{1,0:T(8,128)S(1)}) custom-call(s32[384,128]{1,0:T(8,128)S(1)} %bounds.1.begin_ref, bf16[384,512]{1,0:T(8,128)(2,1)S(1)} %copy-done, f32[384,512]{1,0:T(8,128)S(1)} %get-tuple-element.11.refs_0_, f32[384,512]{1,0:T(8,128)S(1)} %get-tuple-element.12.refs_1_, ...), custom_call_target="tpu_custom_call" | custom-call | flops 452984832 | bytes 393216 | tf_op jit(solution)/shard_map/attend1/pallas_call | solution.py:213
  69.6 0.0 collective-permute-done.4.refs_3_
  69.6 2.0 %attend2.1.refs_0_ = bf16[400,512]{1,0:T(8,128)(2,1)S(1)} custom-call(s32[384,128]{1,0:T(8,128)S(1)} %bounds.1.begin_ref, bf16[384,512]{1,0:T(8,128)(2,1)S(1)} %copy-done, f32[384,512]{1,0:T(8,128)S(1)} %get-tuple-element.14.refs_0_, f32[384,512]{1,0:T(8,128)S(1)} %get-tuple-element.15.refs_1_, f32[384,128]{1,0:T(8,128)S(1)} %get-tuple-element.16.refs_2_, ...), custom_call_target="tpu_custom_call" | custom-call | flops 377487360 | bytes 393216 | tf_op jit(solution)/shard_map/attend2/pallas_call | solution.py:213
  71.7 4.9 %collective-permute-start.7 = (bf16[400,512]{1,0:T(8,128)(2,1)S(1)}, bf16[400,512]{1,0:T(8,128)(2,1)S(1)}, u32[]{:S(2)}, u32[]{:S(2)}) collective-permute-start(bf16[400,512]{1,0:T(8,128)(2,1)S(1)} %attend2.1.refs_0_), channel_id=1, source_target_pairs={{0,768},{256,0},{512,256},{768,512},{1,769},{257,1},{513,257},{769... | collective-permute-start | bytes 1228808 | tf_op jit(solution)/shard_map/ppermute | solution.py:34
  76.6 2.5 %collective-permute-start.6 = (bf16[400,512]{1,0:T(8,128)(2,1)S(1)}, bf16[400,512]{1,0:T(8,128)(2,1)S(1)}, u32[]{:S(2)}, u32[]{:S(2)}) collective-permute-start(bf16[400,512]{1,0:T(8,128)(2,1)S(1)} %attend2.1.refs_0_), channel_id=1, source_target_pairs={{0,512},{256,768},{512,0},{768,256},{1,513},{257,769},{513,1},{769... | collective-permute-start | bytes 1228808 | tf_op jit(solution)/shard_map/ppermute | solution.py:34
  79.1 2.9 %collective-permute-start.5 = (bf16[400,512]{1,0:T(8,128)(2,1)S(1)}, bf16[400,512]{1,0:T(8,128)(2,1)S(1)}, u32[]{:S(2)}, u32[]{:S(2)}) collective-permute-start(bf16[400,512]{1,0:T(8,128)(2,1)S(1)} %attend2.1.refs_0_), channel_id=1, source_target_pairs={{0,256},{256,512},{512,768},{768,0},{1,257},{257,513},{513,769},{7... | collective-permute-start | bytes 1228808 | tf_op jit(solution)/shard_map/ppermute | solution.py:34
  82.0 5.9 %collective-permute-done.7.refs_3_ = bf16[400,512]{1,0:T(8,128)(2,1)S(1)} collective-permute-done((bf16[400,512]{1,0:T(8,128)(2,1)S(1)}, bf16[400,512]{1,0:T(8,128)(2,1)S(1)}, u32[]{:S(2)}, u32[]{:S(2)}) %collective-permute-start.7) | collective-permute-done | bytes 409632 | tf_op jit(solution)/shard_map/ppermute | solution.py:34
  87.9 1.4 %collective-permute-done.6.refs_2_ = bf16[400,512]{1,0:T(8,128)(2,1)S(1)} collective-permute-done((bf16[400,512]{1,0:T(8,128)(2,1)S(1)}, bf16[400,512]{1,0:T(8,128)(2,1)S(1)}, u32[]{:S(2)}, u32[]{:S(2)}) %collective-permute-start.6) | collective-permute-done | bytes 409632 | tf_op jit(solution)/shard_map/ppermute | solution.py:34
  89.3 4.2 %collective-permute-done.5.refs_1_ = bf16[400,512]{1,0:T(8,128)(2,1)S(1)} collective-permute-done((bf16[400,512]{1,0:T(8,128)(2,1)S(1)}, bf16[400,512]{1,0:T(8,128)(2,1)S(1)}, u32[]{:S(2)}, u32[]{:S(2)}) %collective-permute-start.5) | collective-permute-done | bytes 409632 | tf_op jit(solution)/shard_map/ppermute | solution.py:34
  93.5 1.8 %merge.1 = bf16[384,512]{1,0:T(8,128)(2,1)} custom-call(bf16[400,512]{1,0:T(8,128)(2,1)S(1)} %attend2.1.refs_0_, bf16[400,512]{1,0:T(8,128)(2,1)S(1)} %collective-permute-done.5.refs_1_, bf16[400,512]{1,0:T(8,128)(2,1)S(1)} %collective-permute-done.6.refs_2_, bf16[400,512]{1,0:T(8,128)(2,1)S(1)} %collective-permute-done.7.refs_3_), custom_call_target="tpu_custom_call" | custom-call | tf_op jit(solution)/shard_map/merge/pallas_call | solution.py:226
  (6 shorter events, 0.0 us)
Async XLA Ops:
  0.0 56.7 %copy-start.1 = (bf16[1,1,96,1,256]{4,2,3,1,0:T(8,128)(2,1)S(1)}, bf16[1,1,96,1,256]{4,2,3,1,0:T(8,128)(2,1)}, u32[]{:S(2)}) copy-start(bf16[1,1,96,1,256]{4,2,3,1,0:T(8,128)(2,1)} %param.4) | copy-start | bytes 147460
  0.0 24.6 %collective-permute-start = (bf16[96,256]{1,0:T(8,128)(2,1)}, bf16[96,256]{1,0:T(8,128)(2,1)S(1)}, u32[]{:S(2)}, u32[]{:S(2)}) collective-permute-start(bf16[96,256]{1,0:T(8,128)(2,1)} %bitcast.1), channel_id=1, source_target_pairs={{0,6},{1,7},{2,8},{3,9},{4,10},{5,11},{6,12},{7,13},{8,14},{9,15},... | collective-permute-start | bytes 147464 | tf_op jit(solution)/shard_map/ppermute | solution.py:34
  24.6 14.2 %collective-permute-start.1 = (bf16[96,256]{1,0:T(8,128)(2,1)S(1)}, bf16[96,256]{1,0:T(8,128)(2,1)S(1)}, u32[]{:S(2)}, u32[]{:S(2)}) collective-permute-start(bf16[96,256]{1,0:T(8,128)(2,1)S(1)} %collective-permute-done.refs_1_), channel_id=1, source_target_pairs={{0,6},{1,7},{2,8},{3,9},{4,10},{5,11},{6,12},{7,13},{8,14},{9,15},... | collective-permute-start | bytes 147464 | tf_op jit(solution)/shard_map/ppermute | solution.py:34
  39.6 17.1 %collective-permute-start.2 = (bf16[288,256]{1,0:T(8,128)(2,1)S(1)}, bf16[288,256]{1,0:T(8,128)(2,1)S(1)}, u32[]{:S(2)}, u32[]{:S(2)}) collective-permute-start(bf16[288,256]{1,0:T(8,128)(2,1)S(1)} %pad_maximum_fusion.2), channel_id=1, source_target_pairs={{0,3},{1,4},{2,5},{3,6},{4,7},{5,8},{6,9},{7,10},{8,11},{9,12},{10... | collective-permute-start | bytes 442376 | tf_op jit(solution)/shard_map/ppermute | solution.py:34
  56.7 7.3 %copy-start.2 = (s32[8]{0:T(128)S(1)}, s32[8]{0:T(128)}, u32[]{:S(2)}) copy-start(s32[8]{0:T(128)} %lengths.1) | copy-start | bytes 100
  56.7 7.9 %copy-start = (bf16[384,512]{1,0:T(8,128)(2,1)S(1)}, bf16[384,512]{1,0:T(8,128)(2,1)}, u32[]{:S(2)}) copy-start(bf16[384,512]{1,0:T(8,128)(2,1)} %q_ref.5) | copy-start | bytes 1179652
  56.7 10.1 %collective-permute-start.3 = (bf16[576,256]{1,0:T(8,128)(2,1)S(1)}, bf16[576,256]{1,0:T(8,128)(2,1)S(1)}, u32[]{:S(2)}, u32[]{:S(2)}) collective-permute-start(bf16[576,256]{1,0:T(8,128)(2,1)S(1)} %pad_maximum_fusion), channel_id=1, source_target_pairs={{0,1},{1,2},{2,3},{3,4},{4,5},{5,6},{6,7},{7,8},{8,9},{9,10},{10,1... | collective-permute-start | bytes 884744 | tf_op jit(solution)/shard_map/ppermute | solution.py:34
  58.8 10.8 %collective-permute-start.4 = (bf16[480,256]{1,0:T(8,128)(2,1)S(1)}, bf16[480,256]{1,0:T(8,128)(2,1)S(1)}, u32[]{:S(2)}, u32[]{:S(2)}) collective-permute-start(bf16[480,256]{1,0:T(8,128)(2,1)S(1)} %pad_maximum_fusion.1), channel_id=1, source_target_pairs={{0,31},{1,0},{2,1},{3,2},{4,3},{5,4},{6,5},{7,6},{8,7},{9,8},{10,9... | collective-permute-start | bytes 737288 | tf_op jit(solution)/shard_map/ppermute | solution.py:34
  71.7 16.2 %collective-permute-start.7 = (bf16[400,512]{1,0:T(8,128)(2,1)S(1)}, bf16[400,512]{1,0:T(8,128)(2,1)S(1)}, u32[]{:S(2)}, u32[]{:S(2)}) collective-permute-start(bf16[400,512]{1,0:T(8,128)(2,1)S(1)} %attend2.1.refs_0_), channel_id=1, source_target_pairs={{0,768},{256,0},{512,256},{768,512},{1,769},{257,1},{513,257},{769... | collective-permute-start | bytes 1228808 | tf_op jit(solution)/shard_map/ppermute | solution.py:34
  76.6 12.7 %collective-permute-start.6 = (bf16[400,512]{1,0:T(8,128)(2,1)S(1)}, bf16[400,512]{1,0:T(8,128)(2,1)S(1)}, u32[]{:S(2)}, u32[]{:S(2)}) collective-permute-start(bf16[400,512]{1,0:T(8,128)(2,1)S(1)} %attend2.1.refs_0_), channel_id=1, source_target_pairs={{0,512},{256,768},{512,0},{768,256},{1,513},{257,769},{513,1},{769... | collective-permute-start | bytes 1228808 | tf_op jit(solution)/shard_map/ppermute | solution.py:34
  79.1 14.4 %collective-permute-start.5 = (bf16[400,512]{1,0:T(8,128)(2,1)S(1)}, bf16[400,512]{1,0:T(8,128)(2,1)S(1)}, u32[]{:S(2)}, u32[]{:S(2)}) collective-permute-start(bf16[400,512]{1,0:T(8,128)(2,1)S(1)} %attend2.1.refs_0_), channel_id=1, source_target_pairs={{0,256},{256,512},{512,768},{768,0},{1,257},{257,513},{513,769},{7... | collective-permute-start | bytes 1228808 | tf_op jit(solution)/shard_map/ppermute | solution.py:34

commit v4 on v3

--- a/solution.py
+++ b/solution.py
@@ -22,7 +22,7 @@
     (1, (0, 6, 12, 3, 9, 15)),
     (-1, (6, 12, 3, 9, 15)),
 )
-STAGES = ((-1, 0, 1, 2), (3,), (4,))
+STAGES = ((-1, 0, 1), (2, 3), (4,))
 
 
 def distances_of(arrival):

time: 95.8 us -> 94 us (0.981); the launches traced: 95.3 us -> 92.6 us
  waiting for transfers between devices: 44.6 us -> 41 us
  starting transfers between devices: 40.3 us -> 41.5 us
    ppermute x8, waiting for transfers between devices: 44.6 us -> 41 us  [shift(): lax.ppermute(value, axis, [(i, (i + by) % count) for i in range(count)])]
    ppermute x8, starting transfers between devices: 40.3 us -> 41.5 us  [shift(): lax.ppermute(value, axis, [(i, (i + by) % count) for i in range(count)])]
  transfers between devices with their start and end apart: 8 -> 8, of which waited for: 6 -> 7; matrix products, arithmetic and copies ran while one was open for 0% -> 0% of each run, Pallas kernels for 6% -> 6%
where the time goes in v4:
time: 94 us; the launch traced here: 92.6 us
  starting transfers between devices  41.5 us (44%)
  waiting for transfers between devices  41 us (44%)
  Pallas kernels  9.06 us (10%)
    ppermute x8, starting transfers between devices, shift(): lax.ppermute(value, axis, [(i, (i + by) % count) for i in range(count)])  41.5 us
    ppermute x8, waiting for transfers between devices, shift(): lax.ppermute(value, axis, [(i, (i + by) % count) for i in range(count)])  41 us
    pallas_call x3, Pallas kernels, stage_call(): pl.pallas_call(functools.partial(stage_kernel, factor, size, key_rows, st...  6.56 us
  transfers between devices with their start and end apart: 8, of which 7 were waited for; matrix products, arithmetic and copies ran while one was open for 0% of the time, Pallas kernels for 6%

profile of v4, /device:TPU:6, one launch (start us, length us, event | category | flops | bytes accessed | tf_op | source)
XLA Modules:
  0.0 92.6 jit_solution(9313012967563424367)
XLA Ops:
  0.0 11.9 %collective-permute-start = (bf16[96,256]{1,0:T(8,128)(2,1)}, bf16[96,256]{1,0:T(8,128)(2,1)S(1)}, u32[]{:S(2)}, u32[]{:S(2)}) collective-permute-start(bf16[96,256]{1,0:T(8,128)(2,1)} %bitcast.1), channel_id=1, source_target_pairs={{0,6},{1,7},{2,8},{3,9},{4,10},{5,11},{6,12},{7,13},{8,14},{9,15},... | collective-permute-start | bytes 147464 | tf_op jit(solution)/shard_map/ppermute | solution.py:34
  11.9 12.7 %collective-permute-done.refs_1_ = bf16[96,256]{1,0:T(8,128)(2,1)S(1)} collective-permute-done((bf16[96,256]{1,0:T(8,128)(2,1)}, bf16[96,256]{1,0:T(8,128)(2,1)S(1)}, u32[]{:S(2)}, u32[]{:S(2)}) %collective-permute-start) | collective-permute-done | bytes 49184 | tf_op jit(solution)/shard_map/ppermute | solution.py:34
  24.6 4.2 %collective-permute-start.1 = (bf16[96,256]{1,0:T(8,128)(2,1)S(1)}, bf16[96,256]{1,0:T(8,128)(2,1)S(1)}, u32[]{:S(2)}, u32[]{:S(2)}) collective-permute-start(bf16[96,256]{1,0:T(8,128)(2,1)S(1)} %collective-permute-done.refs_1_), channel_id=1, source_target_pairs={{0,6},{1,7},{2,8},{3,9},{4,10},{5,11},{6,12},{7,13},{8,14},{9,15},... | collective-permute-start | bytes 147464 | tf_op jit(solution)/shard_map/ppermute | solution.py:34
  28.8 10.0 %collective-permute-done.1.refs_2_ = bf16[96,256]{1,0:T(8,128)(2,1)S(1)} collective-permute-done((bf16[96,256]{1,0:T(8,128)(2,1)S(1)}, bf16[96,256]{1,0:T(8,128)(2,1)S(1)}, u32[]{:S(2)}, u32[]{:S(2)}) %collective-permute-start.1) | collective-permute-done | bytes 49184 | tf_op jit(solution)/shard_map/ppermute | solution.py:34
  38.8 0.8 pad_maximum_fusion.2
  39.6 6.6 %collective-permute-start.2 = (bf16[288,256]{1,0:T(8,128)(2,1)S(1)}, bf16[288,256]{1,0:T(8,128)(2,1)S(1)}, u32[]{:S(2)}, u32[]{:S(2)}) collective-permute-start(bf16[288,256]{1,0:T(8,128)(2,1)S(1)} %pad_maximum_fusion.2), channel_id=1, source_target_pairs={{0,3},{1,4},{2,5},{3,6},{4,7},{5,8},{6,9},{7,10},{8,11},{9,12},{10... | collective-permute-start | bytes 442376 | tf_op jit(solution)/shard_map/ppermute | solution.py:34
  46.3 10.4 %collective-permute-done.2.refs_3_ = bf16[288,256]{1,0:T(8,128)(2,1)S(1)} collective-permute-done((bf16[288,256]{1,0:T(8,128)(2,1)S(1)}, bf16[288,256]{1,0:T(8,128)(2,1)S(1)}, u32[]{:S(2)}, u32[]{:S(2)}) %collective-permute-start.2) | collective-permute-done | bytes 147488 | tf_op jit(solution)/shard_map/ppermute | solution.py:34
  56.7 0.0 copy-start.2
  56.7 0.0 copy-start
  56.7 2.1 %collective-permute-start.3 = (bf16[576,256]{1,0:T(8,128)(2,1)S(1)}, bf16[576,256]{1,0:T(8,128)(2,1)S(1)}, u32[]{:S(2)}, u32[]{:S(2)}) collective-permute-start(bf16[576,256]{1,0:T(8,128)(2,1)S(1)} %pad_maximum_fusion), channel_id=1, source_target_pairs={{0,1},{1,2},{2,3},{3,4},{4,5},{5,6},{6,7},{7,8},{8,9},{9,10},{10,1... | collective-permute-start | bytes 884744 | tf_op jit(solution)/shard_map/ppermute | solution.py:34
  58.8 5.1 %collective-permute-start.4 = (bf16[480,256]{1,0:T(8,128)(2,1)S(1)}, bf16[480,256]{1,0:T(8,128)(2,1)S(1)}, u32[]{:S(2)}, u32[]{:S(2)}) collective-permute-start(bf16[480,256]{1,0:T(8,128)(2,1)S(1)} %pad_maximum_fusion.1), channel_id=1, source_target_pairs={{0,31},{1,0},{2,1},{3,2},{4,3},{5,4},{6,5},{7,6},{8,7},{9,8},{10,9... | collective-permute-start | bytes 737288 | tf_op jit(solution)/shard_map/ppermute | solution.py:34
  64.0 0.7 bounds.1.begin_ref
  64.7 1.7 %attend0.1 = (f32[384,512]{1,0:T(8,128)S(1)}, f32[384,512]{1,0:T(8,128)S(1)}, f32[384,128]{1,0:T(8,128)S(1)}) custom-call(s32[384,128]{1,0:T(8,128)S(1)} %bounds.1.begin_ref, bf16[384,512]{1,0:T(8,128)(2,1)S(1)} %copy-done, bf16[96,256]{1,0:T(8,128)(2,1)S(1)} %bitcast.4, bf16[96,256]{1,0:T(8,128)(2,1)S(1)} %collective-permute-done.refs_1_, ...), custom_call_target="tpu_custom_call" | custom-call | flops 226492416 | bytes 393216 | tf_op jit(solution)/shard_map/attend0/pallas_call | solution.py:213
  66.3 0.4 collective-permute-done.3.refs_4_
  66.7 2.8 %attend1.1 = (f32[384,512]{1,0:T(8,128)S(1)}, f32[384,512]{1,0:T(8,128)S(1)}, f32[384,128]{1,0:T(8,128)S(1)}) custom-call(s32[384,128]{1,0:T(8,128)S(1)} %bounds.1.begin_ref, bf16[384,512]{1,0:T(8,128)(2,1)S(1)} %copy-done, f32[384,512]{1,0:T(8,128)S(1)} %get-tuple-element.11.refs_0_, f32[384,512]{1,0:T(8,128)S(1)} %get-tuple-element.12.refs_1_, ...), custom_call_target="tpu_custom_call" | custom-call | flops 679477248 | bytes 393216 | tf_op jit(solution)/shard_map/attend1/pallas_call | solution.py:213
  69.5 0.0 collective-permute-done.4.refs_3_
  69.6 2.1 %attend2.1.refs_0_ = bf16[400,512]{1,0:T(8,128)(2,1)S(1)} custom-call(s32[384,128]{1,0:T(8,128)S(1)} %bounds.1.begin_ref, bf16[384,512]{1,0:T(8,128)(2,1)S(1)} %copy-done, f32[384,512]{1,0:T(8,128)S(1)} %get-tuple-element.14.refs_0_, f32[384,512]{1,0:T(8,128)S(1)} %get-tuple-element.15.refs_1_, f32[384,128]{1,0:T(8,128)S(1)} %get-tuple-element.16.refs_2_, ...), custom_call_target="tpu_custom_call" | custom-call | flops 377487360 | bytes 393216 | tf_op jit(solution)/shard_map/attend2/pallas_call | solution.py:213
  71.6 3.5 %collective-permute-start.5 = (bf16[400,512]{1,0:T(8,128)(2,1)S(1)}, bf16[400,512]{1,0:T(8,128)(2,1)S(1)}, u32[]{:S(2)}, u32[]{:S(2)}) collective-permute-start(bf16[400,512]{1,0:T(8,128)(2,1)S(1)} %attend2.1.refs_0_), channel_id=1, source_target_pairs={{0,256},{256,512},{512,768},{768,0},{1,257},{257,513},{513,769},{7... | collective-permute-start | bytes 1228808 | tf_op jit(solution)/shard_map/ppermute | solution.py:34
  75.1 4.8 %collective-permute-start.6 = (bf16[400,512]{1,0:T(8,128)(2,1)S(1)}, bf16[400,512]{1,0:T(8,128)(2,1)S(1)}, u32[]{:S(2)}, u32[]{:S(2)}) collective-permute-start(bf16[400,512]{1,0:T(8,128)(2,1)S(1)} %attend2.1.refs_0_), channel_id=1, source_target_pairs={{0,512},{256,768},{512,0},{768,256},{1,513},{257,769},{513,1},{769... | collective-permute-start | bytes 1228808 | tf_op jit(solution)/shard_map/ppermute | solution.py:34
  79.9 3.3 %collective-permute-start.7 = (bf16[400,512]{1,0:T(8,128)(2,1)S(1)}, bf16[400,512]{1,0:T(8,128)(2,1)S(1)}, u32[]{:S(2)}, u32[]{:S(2)}) collective-permute-start(bf16[400,512]{1,0:T(8,128)(2,1)S(1)} %attend2.1.refs_0_), channel_id=1, source_target_pairs={{0,768},{256,0},{512,256},{768,512},{1,769},{257,1},{513,257},{769... | collective-permute-start | bytes 1228808 | tf_op jit(solution)/shard_map/ppermute | solution.py:34
  83.2 1.8 %collective-permute-done.5.refs_1_ = bf16[400,512]{1,0:T(8,128)(2,1)S(1)} collective-permute-done((bf16[400,512]{1,0:T(8,128)(2,1)S(1)}, bf16[400,512]{1,0:T(8,128)(2,1)S(1)}, u32[]{:S(2)}, u32[]{:S(2)}) %collective-permute-start.5) | collective-permute-done | bytes 409632 | tf_op jit(solution)/shard_map/ppermute | solution.py:34
  85.0 4.4 %collective-permute-done.6.refs_2_ = bf16[400,512]{1,0:T(8,128)(2,1)S(1)} collective-permute-done((bf16[400,512]{1,0:T(8,128)(2,1)S(1)}, bf16[400,512]{1,0:T(8,128)(2,1)S(1)}, u32[]{:S(2)}, u32[]{:S(2)}) %collective-permute-start.6) | collective-permute-done | bytes 409632 | tf_op jit(solution)/shard_map/ppermute | solution.py:34
  89.4 1.3 %collective-permute-done.7.refs_3_ = bf16[400,512]{1,0:T(8,128)(2,1)S(1)} collective-permute-done((bf16[400,512]{1,0:T(8,128)(2,1)S(1)}, bf16[400,512]{1,0:T(8,128)(2,1)S(1)}, u32[]{:S(2)}, u32[]{:S(2)}) %collective-permute-start.7) | collective-permute-done | bytes 409632 | tf_op jit(solution)/shard_map/ppermute | solution.py:34
  90.7 1.8 %merge.1 = bf16[384,512]{1,0:T(8,128)(2,1)} custom-call(bf16[400,512]{1,0:T(8,128)(2,1)S(1)} %attend2.1.refs_0_, bf16[400,512]{1,0:T(8,128)(2,1)S(1)} %collective-permute-done.5.refs_1_, bf16[400,512]{1,0:T(8,128)(2,1)S(1)} %collective-permute-done.6.refs_2_, bf16[400,512]{1,0:T(8,128)(2,1)S(1)} %collective-permute-done.7.refs_3_), custom_call_target="tpu_custom_call" | custom-call | tf_op jit(solution)/shard_map/merge/pallas_call | solution.py:226
  (6 shorter events, 0.0 us)
Async XLA Ops:
  0.0 56.7 %copy-start.1 = (bf16[1,1,96,1,256]{4,2,3,1,0:T(8,128)(2,1)S(1)}, bf16[1,1,96,1,256]{4,2,3,1,0:T(8,128)(2,1)}, u32[]{:S(2)}) copy-start(bf16[1,1,96,1,256]{4,2,3,1,0:T(8,128)(2,1)} %param.4) | copy-start | bytes 147460
  0.0 24.6 %collective-permute-start = (bf16[96,256]{1,0:T(8,128)(2,1)}, bf16[96,256]{1,0:T(8,128)(2,1)S(1)}, u32[]{:S(2)}, u32[]{:S(2)}) collective-permute-start(bf16[96,256]{1,0:T(8,128)(2,1)} %bitcast.1), channel_id=1, source_target_pairs={{0,6},{1,7},{2,8},{3,9},{4,10},{5,11},{6,12},{7,13},{8,14},{9,15},... | collective-permute-start | bytes 147464 | tf_op jit(solution)/shard_map/ppermute | solution.py:34
  24.6 14.2 %collective-permute-start.1 = (bf16[96,256]{1,0:T(8,128)(2,1)S(1)}, bf16[96,256]{1,0:T(8,128)(2,1)S(1)}, u32[]{:S(2)}, u32[]{:S(2)}) collective-permute-start(bf16[96,256]{1,0:T(8,128)(2,1)S(1)} %collective-permute-done.refs_1_), channel_id=1, source_target_pairs={{0,6},{1,7},{2,8},{3,9},{4,10},{5,11},{6,12},{7,13},{8,14},{9,15},... | collective-permute-start | bytes 147464 | tf_op jit(solution)/shard_map/ppermute | solution.py:34
  39.6 17.1 %collective-permute-start.2 = (bf16[288,256]{1,0:T(8,128)(2,1)S(1)}, bf16[288,256]{1,0:T(8,128)(2,1)S(1)}, u32[]{:S(2)}, u32[]{:S(2)}) collective-permute-start(bf16[288,256]{1,0:T(8,128)(2,1)S(1)} %pad_maximum_fusion.2), channel_id=1, source_target_pairs={{0,3},{1,4},{2,5},{3,6},{4,7},{5,8},{6,9},{7,10},{8,11},{9,12},{10... | collective-permute-start | bytes 442376 | tf_op jit(solution)/shard_map/ppermute | solution.py:34
  56.7 7.3 %copy-start.2 = (s32[8]{0:T(128)S(1)}, s32[8]{0:T(128)}, u32[]{:S(2)}) copy-start(s32[8]{0:T(128)} %lengths.1) | copy-start | bytes 100
  56.7 7.9 %copy-start = (bf16[384,512]{1,0:T(8,128)(2,1)S(1)}, bf16[384,512]{1,0:T(8,128)(2,1)}, u32[]{:S(2)}) copy-start(bf16[384,512]{1,0:T(8,128)(2,1)} %q_ref.5) | copy-start | bytes 1179652
  56.7 10.0 %collective-permute-start.3 = (bf16[576,256]{1,0:T(8,128)(2,1)S(1)}, bf16[576,256]{1,0:T(8,128)(2,1)S(1)}, u32[]{:S(2)}, u32[]{:S(2)}) collective-permute-start(bf16[576,256]{1,0:T(8,128)(2,1)S(1)} %pad_maximum_fusion), channel_id=1, source_target_pairs={{0,1},{1,2},{2,3},{3,4},{4,5},{5,6},{6,7},{7,8},{8,9},{9,10},{10,1... | collective-permute-start | bytes 884744 | tf_op jit(solution)/shard_map/ppermute | solution.py:34
  58.8 10.7 %collective-permute-start.4 = (bf16[480,256]{1,0:T(8,128)(2,1)S(1)}, bf16[480,256]{1,0:T(8,128)(2,1)S(1)}, u32[]{:S(2)}, u32[]{:S(2)}) collective-permute-start(bf16[480,256]{1,0:T(8,128)(2,1)S(1)} %pad_maximum_fusion.1), channel_id=1, source_target_pairs={{0,31},{1,0},{2,1},{3,2},{4,3},{5,4},{6,5},{7,6},{8,7},{9,8},{10,9... | collective-permute-start | bytes 737288 | tf_op jit(solution)/shard_map/ppermute | solution.py:34
  71.6 13.4 %collective-permute-start.5 = (bf16[400,512]{1,0:T(8,128)(2,1)S(1)}, bf16[400,512]{1,0:T(8,128)(2,1)S(1)}, u32[]{:S(2)}, u32[]{:S(2)}) collective-permute-start(bf16[400,512]{1,0:T(8,128)(2,1)S(1)} %attend2.1.refs_0_), channel_id=1, source_target_pairs={{0,256},{256,512},{512,768},{768,0},{1,257},{257,513},{513,769},{7... | collective-permute-start | bytes 1228808 | tf_op jit(solution)/shard_map/ppermute | solution.py:34
  75.1 14.3 %collective-permute-start.6 = (bf16[400,512]{1,0:T(8,128)(2,1)S(1)}, bf16[400,512]{1,0:T(8,128)(2,1)S(1)}, u32[]{:S(2)}, u32[]{:S(2)}) collective-permute-start(bf16[400,512]{1,0:T(8,128)(2,1)S(1)} %attend2.1.refs_0_), channel_id=1, source_target_pairs={{0,512},{256,768},{512,0},{768,256},{1,513},{257,769},{513,1},{769... | collective-permute-start | bytes 1228808 | tf_op jit(solution)/shard_map/ppermute | solution.py:34
  79.9 10.8 %collective-permute-start.7 = (bf16[400,512]{1,0:T(8,128)(2,1)S(1)}, bf16[400,512]{1,0:T(8,128)(2,1)S(1)}, u32[]{:S(2)}, u32[]{:S(2)}) collective-permute-start(bf16[400,512]{1,0:T(8,128)(2,1)S(1)} %attend2.1.refs_0_), channel_id=1, source_target_pairs={{0,768},{256,0},{512,256},{768,512},{1,769},{257,1},{513,257},{769... | collective-permute-start | bytes 1228808 | tf_op jit(solution)/shard_map/ppermute | solution.py:34

commit v5 on v4

--- a/solution.py
+++ b/solution.py
@@ -23,6 +23,7 @@
     (-1, (6, 12, 3, 9, 15)),
 )
 STAGES = ((-1, 0, 1), (2, 3), (4,))
+AHEAD = 3
 
 
 def distances_of(arrival):
@@ -241,20 +242,23 @@
     own = key_values.reshape(key_rows, 2 * size)
     held = {0: (own, 0)}
     arrived = []
-    for by, carried in PLAN:
+    begin = bounds_call(lengths, rows)
+    for index, (by, carried) in enumerate(PLAN):
         cargo = joined([held[d] for d in carried], key_rows)
+        if index == AHEAD:
+            chunks = [own, *(arrived[arrival] for arrival in STAGES[0][1:])]
+            state = stage_call(factor, size, key_rows, 0, begin, queries, (), chunks)
+            cargo, state = lax.optimization_barrier((cargo, state))
         result = shift(cargo, "tok", by, tiles)
         arrived.append(result)
         for i, d in enumerate(carried):
             held[d] = (cargo, i * key_rows)
             held[d + by] = (result, i * key_rows)
-    begin = bounds_call(lengths, rows)
-    state = ()
-    for stage, arrivals in enumerate(STAGES):
-        chunks = [own if arrival < 0 else arrived[arrival] for arrival in arrivals]
+    for stage, arrivals in tuple(enumerate(STAGES))[1:]:
+        chunks = [arrived[arrival] for arrival in arrivals]
         state = stage_call(factor, size, key_rows, stage, begin, queries, state, chunks)
     part = state
-    parts = [part] + [shift(part, "section", by, splits) for by in range(1, splits)]
+    parts = [part] + [shift(part, "section", by, splits) for by in reversed(range(1, splits))]
     return merge_call(size, rows, parts)
 
 

time: 94 us -> 93.9 us (level)
  no operation moved by 1% of the time
where the time goes in v5:
time: 93.9 us; the launch traced here: 92.5 us
  starting transfers between devices  41.4 us (44%)
  waiting for transfers between devices  41.1 us (44%)
  Pallas kernels  9.03 us (10%)
    ppermute x8, starting transfers between devices, shift(): lax.ppermute(value, axis, [(i, (i + by) % count) for i in range(count)])  41.4 us
    ppermute x8, waiting for transfers between devices, shift(): lax.ppermute(value, axis, [(i, (i + by) % count) for i in range(count)])  41.1 us
    pallas_call x3, Pallas kernels, stage_call(): pl.pallas_call(functools.partial(stage_kernel, factor, size, key_rows, st...  6.52 us
  transfers between devices with their start and end apart: 8, of which 7 were waited for; matrix products, arithmetic and copies ran while one was open for 0% of the time, Pallas kernels for 6%

profile of v5, /device:TPU:6, one launch (start us, length us, event | category | flops | bytes accessed | tf_op | source)
XLA Modules:
  0.0 92.5 jit_solution(2896437938322771142)
XLA Ops:
  0.0 11.9 %collective-permute-start = (bf16[96,256]{1,0:T(8,128)(2,1)}, bf16[96,256]{1,0:T(8,128)(2,1)S(1)}, u32[]{:S(2)}, u32[]{:S(2)}) collective-permute-start(bf16[96,256]{1,0:T(8,128)(2,1)} %bitcast.1), channel_id=1, source_target_pairs={{0,6},{1,7},{2,8},{3,9},{4,10},{5,11},{6,12},{7,13},{8,14},{9,15},... | collective-permute-start | bytes 147464 | tf_op jit(solution)/shard_map/ppermute | solution.py:35
  11.9 12.7 %collective-permute-done.refs_1_ = bf16[96,256]{1,0:T(8,128)(2,1)S(1)} collective-permute-done((bf16[96,256]{1,0:T(8,128)(2,1)}, bf16[96,256]{1,0:T(8,128)(2,1)S(1)}, u32[]{:S(2)}, u32[]{:S(2)}) %collective-permute-start) | collective-permute-done | bytes 49184 | tf_op jit(solution)/shard_map/ppermute | solution.py:35
  24.6 4.2 %collective-permute-start.1 = (bf16[96,256]{1,0:T(8,128)(2,1)S(1)}, bf16[96,256]{1,0:T(8,128)(2,1)S(1)}, u32[]{:S(2)}, u32[]{:S(2)}) collective-permute-start(bf16[96,256]{1,0:T(8,128)(2,1)S(1)} %collective-permute-done.refs_1_), channel_id=1, source_target_pairs={{0,6},{1,7},{2,8},{3,9},{4,10},{5,11},{6,12},{7,13},{8,14},{9,15},... | collective-permute-start | bytes 147464 | tf_op jit(solution)/shard_map/ppermute | solution.py:35
  28.8 10.0 %collective-permute-done.1.refs_2_ = bf16[96,256]{1,0:T(8,128)(2,1)S(1)} collective-permute-done((bf16[96,256]{1,0:T(8,128)(2,1)S(1)}, bf16[96,256]{1,0:T(8,128)(2,1)S(1)}, u32[]{:S(2)}, u32[]{:S(2)}) %collective-permute-start.1) | collective-permute-done | bytes 49184 | tf_op jit(solution)/shard_map/ppermute | solution.py:35
  38.8 0.8 pad_maximum_fusion.1
  39.6 0.0 copy-start.1
  39.6 6.7 %collective-permute-start.2 = (bf16[288,256]{1,0:T(8,128)(2,1)S(1)}, bf16[288,256]{1,0:T(8,128)(2,1)S(1)}, u32[]{:S(2)}, u32[]{:S(2)}) collective-permute-start(bf16[288,256]{1,0:T(8,128)(2,1)S(1)} %pad_maximum_fusion.1), channel_id=1, source_target_pairs={{0,3},{1,4},{2,5},{3,6},{4,7},{5,8},{6,9},{7,10},{8,11},{9,12},{10... | collective-permute-start | bytes 442376 | tf_op jit(solution)/shard_map/ppermute | solution.py:35
  46.4 0.0 copy-done.2
  46.4 0.7 bounds.1.begin_ref
  47.1 1.6 %attend0.1 = (f32[384,512]{1,0:T(8,128)S(1)}, f32[384,512]{1,0:T(8,128)S(1)}, f32[384,128]{1,0:T(8,128)S(1)}) custom-call(s32[384,128]{1,0:T(8,128)S(1)} %bounds.1.begin_ref, bf16[384,512]{1,0:T(8,128)(2,1)S(1)} %copy-done, bf16[96,256]{1,0:T(8,128)(2,1)S(1)} %bitcast.3, bf16[96,256]{1,0:T(8,128)(2,1)S(1)} %collective-permute-done.refs_1_, ...), custom_call_target="tpu_custom_call" | custom-call | flops 226492416 | bytes 393216 | tf_op jit(solution)/shard_map/attend0/pallas_call | solution.py:214
  48.7 8.1 %collective-permute-done.2.refs_3_ = bf16[288,256]{1,0:T(8,128)(2,1)S(1)} collective-permute-done((bf16[288,256]{1,0:T(8,128)(2,1)S(1)}, bf16[288,256]{1,0:T(8,128)(2,1)S(1)}, u32[]{:S(2)}, u32[]{:S(2)}) %collective-permute-start.2) | collective-permute-done | bytes 147488 | tf_op jit(solution)/shard_map/ppermute | solution.py:35
  56.8 1.9 %collective-permute-start.3 = (bf16[576,256]{1,0:T(8,128)(2,1)S(1)}, bf16[576,256]{1,0:T(8,128)(2,1)S(1)}, u32[]{:S(2)}, u32[]{:S(2)}) collective-permute-start(bf16[576,256]{1,0:T(8,128)(2,1)S(1)} %pad_maximum_fusion), channel_id=1, source_target_pairs={{0,1},{1,2},{2,3},{3,4},{4,5},{5,6},{6,7},{7,8},{8,9},{9,10},{10,1... | collective-permute-start | bytes 884744 | tf_op jit(solution)/shard_map/ppermute | solution.py:35
  58.8 5.1 %collective-permute-start.4 = (bf16[480,256]{1,0:T(8,128)(2,1)S(1)}, bf16[480,256]{1,0:T(8,128)(2,1)S(1)}, u32[]{:S(2)}, u32[]{:S(2)}) collective-permute-start(bf16[480,256]{1,0:T(8,128)(2,1)S(1)} %slice.3), channel_id=1, source_target_pairs={{0,31},{1,0},{2,1},{3,2},{4,3},{5,4},{6,5},{7,6},{8,7},{9,8},{10,9... | collective-permute-start | bytes 737288 | tf_op jit(solution)/shard_map/ppermute | solution.py:35
  63.9 2.7 %collective-permute-done.3.refs_4_ = bf16[576,256]{1,0:T(8,128)(2,1)S(1)} collective-permute-done((bf16[576,256]{1,0:T(8,128)(2,1)S(1)}, bf16[576,256]{1,0:T(8,128)(2,1)S(1)}, u32[]{:S(2)}, u32[]{:S(2)}) %collective-permute-start.3) | collective-permute-done | bytes 294944 | tf_op jit(solution)/shard_map/ppermute | solution.py:35
  66.7 2.8 %attend1.1 = (f32[384,512]{1,0:T(8,128)S(1)}, f32[384,512]{1,0:T(8,128)S(1)}, f32[384,128]{1,0:T(8,128)S(1)}) custom-call(s32[384,128]{1,0:T(8,128)S(1)} %bounds.1.begin_ref, bf16[384,512]{1,0:T(8,128)(2,1)S(1)} %copy-done, f32[384,512]{1,0:T(8,128)S(1)} %get-tuple-element.18.refs_0_, f32[384,512]{1,0:T(8,128)S(1)} %get-tuple-element.19.refs_1_, ...), custom_call_target="tpu_custom_call" | custom-call | flops 679477248 | bytes 393216 | tf_op jit(solution)/shard_map/attend1/pallas_call | solution.py:214
  69.5 0.0 collective-permute-done.4.refs_3_
  69.5 2.0 %attend2.1.refs_0_ = bf16[400,512]{1,0:T(8,128)(2,1)S(1)} custom-call(s32[384,128]{1,0:T(8,128)S(1)} %bounds.1.begin_ref, bf16[384,512]{1,0:T(8,128)(2,1)S(1)} %copy-done, f32[384,512]{1,0:T(8,128)S(1)} %get-tuple-element.22.refs_0_, f32[384,512]{1,0:T(8,128)S(1)} %get-tuple-element.23.refs_1_, f32[384,128]{1,0:T(8,128)S(1)} %get-tuple-element.24.refs_2_, ...), custom_call_target="tpu_custom_call" | custom-call | flops 377487360 | bytes 393216 | tf_op jit(solution)/shard_map/attend2/pallas_call | solution.py:214
  71.6 3.5 %collective-permute-start.7 = (bf16[400,512]{1,0:T(8,128)(2,1)S(1)}, bf16[400,512]{1,0:T(8,128)(2,1)S(1)}, u32[]{:S(2)}, u32[]{:S(2)}) collective-permute-start(bf16[400,512]{1,0:T(8,128)(2,1)S(1)} %attend2.1.refs_0_), channel_id=1, source_target_pairs={{0,256},{256,512},{512,768},{768,0},{1,257},{257,513},{513,769},{7... | collective-permute-start | bytes 1228808 | tf_op jit(solution)/shard_map/ppermute | solution.py:35
  75.1 4.8 %collective-permute-start.6 = (bf16[400,512]{1,0:T(8,128)(2,1)S(1)}, bf16[400,512]{1,0:T(8,128)(2,1)S(1)}, u32[]{:S(2)}, u32[]{:S(2)}) collective-permute-start(bf16[400,512]{1,0:T(8,128)(2,1)S(1)} %attend2.1.refs_0_), channel_id=1, source_target_pairs={{0,512},{256,768},{512,0},{768,256},{1,513},{257,769},{513,1},{769... | collective-permute-start | bytes 1228808 | tf_op jit(solution)/shard_map/ppermute | solution.py:35
  79.9 3.3 %collective-permute-start.5 = (bf16[400,512]{1,0:T(8,128)(2,1)S(1)}, bf16[400,512]{1,0:T(8,128)(2,1)S(1)}, u32[]{:S(2)}, u32[]{:S(2)}) collective-permute-start(bf16[400,512]{1,0:T(8,128)(2,1)S(1)} %attend2.1.refs_0_), channel_id=1, source_target_pairs={{0,768},{256,0},{512,256},{768,512},{1,769},{257,1},{513,257},{769... | collective-permute-start | bytes 1228808 | tf_op jit(solution)/shard_map/ppermute | solution.py:35
  83.1 1.8 %collective-permute-done.7.refs_3_ = bf16[400,512]{1,0:T(8,128)(2,1)S(1)} collective-permute-done((bf16[400,512]{1,0:T(8,128)(2,1)S(1)}, bf16[400,512]{1,0:T(8,128)(2,1)S(1)}, u32[]{:S(2)}, u32[]{:S(2)}) %collective-permute-start.7) | collective-permute-done | bytes 409632 | tf_op jit(solution)/shard_map/ppermute | solution.py:35
  85.0 4.4 %collective-permute-done.6.refs_2_ = bf16[400,512]{1,0:T(8,128)(2,1)S(1)} collective-permute-done((bf16[400,512]{1,0:T(8,128)(2,1)S(1)}, bf16[400,512]{1,0:T(8,128)(2,1)S(1)}, u32[]{:S(2)}, u32[]{:S(2)}) %collective-permute-start.6) | collective-permute-done | bytes 409632 | tf_op jit(solution)/shard_map/ppermute | solution.py:35
  89.4 1.3 %collective-permute-done.5.refs_1_ = bf16[400,512]{1,0:T(8,128)(2,1)S(1)} collective-permute-done((bf16[400,512]{1,0:T(8,128)(2,1)S(1)}, bf16[400,512]{1,0:T(8,128)(2,1)S(1)}, u32[]{:S(2)}, u32[]{:S(2)}) %collective-permute-start.5) | collective-permute-done | bytes 409632 | tf_op jit(solution)/shard_map/ppermute | solution.py:35
  90.7 1.8 %merge.1 = bf16[384,512]{1,0:T(8,128)(2,1)} custom-call(bf16[400,512]{1,0:T(8,128)(2,1)S(1)} %attend2.1.refs_0_, bf16[400,512]{1,0:T(8,128)(2,1)S(1)} %collective-permute-done.5.refs_1_, bf16[400,512]{1,0:T(8,128)(2,1)S(1)} %collective-permute-done.6.refs_2_, bf16[400,512]{1,0:T(8,128)(2,1)S(1)} %collective-permute-done.7.refs_3_), custom_call_target="tpu_custom_call" | custom-call | tf_op jit(solution)/shard_map/merge/pallas_call | solution.py:227
  (6 shorter events, 0.0 us)
Async XLA Ops:
  0.0 46.4 %copy-start.2 = (s32[8]{0:T(128)S(1)}, s32[8]{0:T(128)}, u32[]{:S(2)}) copy-start(s32[8]{0:T(128)} %lengths.1) | copy-start | bytes 100
  0.0 47.1 %copy-start = (bf16[384,512]{1,0:T(8,128)(2,1)S(1)}, bf16[384,512]{1,0:T(8,128)(2,1)}, u32[]{:S(2)}) copy-start(bf16[384,512]{1,0:T(8,128)(2,1)} %q_ref.5) | copy-start | bytes 1179652
  0.0 24.6 %collective-permute-start = (bf16[96,256]{1,0:T(8,128)(2,1)}, bf16[96,256]{1,0:T(8,128)(2,1)S(1)}, u32[]{:S(2)}, u32[]{:S(2)}) collective-permute-start(bf16[96,256]{1,0:T(8,128)(2,1)} %bitcast.1), channel_id=1, source_target_pairs={{0,6},{1,7},{2,8},{3,9},{4,10},{5,11},{6,12},{7,13},{8,14},{9,15},... | collective-permute-start | bytes 147464 | tf_op jit(solution)/shard_map/ppermute | solution.py:35
  24.6 14.2 %collective-permute-start.1 = (bf16[96,256]{1,0:T(8,128)(2,1)S(1)}, bf16[96,256]{1,0:T(8,128)(2,1)S(1)}, u32[]{:S(2)}, u32[]{:S(2)}) collective-permute-start(bf16[96,256]{1,0:T(8,128)(2,1)S(1)} %collective-permute-done.refs_1_), channel_id=1, source_target_pairs={{0,6},{1,7},{2,8},{3,9},{4,10},{5,11},{6,12},{7,13},{8,14},{9,15},... | collective-permute-start | bytes 147464 | tf_op jit(solution)/shard_map/ppermute | solution.py:35
  39.6 7.5 %copy-start.1 = (bf16[1,1,96,1,256]{4,2,3,1,0:T(8,128)(2,1)S(1)}, bf16[1,1,96,1,256]{4,2,3,1,0:T(8,128)(2,1)}, u32[]{:S(2)}) copy-start(bf16[1,1,96,1,256]{4,2,3,1,0:T(8,128)(2,1)} %param.4) | copy-start | bytes 147460
  39.6 17.2 %collective-permute-start.2 = (bf16[288,256]{1,0:T(8,128)(2,1)S(1)}, bf16[288,256]{1,0:T(8,128)(2,1)S(1)}, u32[]{:S(2)}, u32[]{:S(2)}) collective-permute-start(bf16[288,256]{1,0:T(8,128)(2,1)S(1)} %pad_maximum_fusion.1), channel_id=1, source_target_pairs={{0,3},{1,4},{2,5},{3,6},{4,7},{5,8},{6,9},{7,10},{8,11},{9,12},{10... | collective-permute-start | bytes 442376 | tf_op jit(solution)/shard_map/ppermute | solution.py:35
  56.8 9.8 %collective-permute-start.3 = (bf16[576,256]{1,0:T(8,128)(2,1)S(1)}, bf16[576,256]{1,0:T(8,128)(2,1)S(1)}, u32[]{:S(2)}, u32[]{:S(2)}) collective-permute-start(bf16[576,256]{1,0:T(8,128)(2,1)S(1)} %pad_maximum_fusion), channel_id=1, source_target_pairs={{0,1},{1,2},{2,3},{3,4},{4,5},{5,6},{6,7},{7,8},{8,9},{9,10},{10,1... | collective-permute-start | bytes 884744 | tf_op jit(solution)/shard_map/ppermute | solution.py:35
  58.8 10.7 %collective-permute-start.4 = (bf16[480,256]{1,0:T(8,128)(2,1)S(1)}, bf16[480,256]{1,0:T(8,128)(2,1)S(1)}, u32[]{:S(2)}, u32[]{:S(2)}) collective-permute-start(bf16[480,256]{1,0:T(8,128)(2,1)S(1)} %slice.3), channel_id=1, source_target_pairs={{0,31},{1,0},{2,1},{3,2},{4,3},{5,4},{6,5},{7,6},{8,7},{9,8},{10,9... | collective-permute-start | bytes 737288 | tf_op jit(solution)/shard_map/ppermute | solution.py:35
  71.6 13.4 %collective-permute-start.7 = (bf16[400,512]{1,0:T(8,128)(2,1)S(1)}, bf16[400,512]{1,0:T(8,128)(2,1)S(1)}, u32[]{:S(2)}, u32[]{:S(2)}) collective-permute-start(bf16[400,512]{1,0:T(8,128)(2,1)S(1)} %attend2.1.refs_0_), channel_id=1, source_target_pairs={{0,256},{256,512},{512,768},{768,0},{1,257},{257,513},{513,769},{7... | collective-permute-start | bytes 1228808 | tf_op jit(solution)/shard_map/ppermute | solution.py:35
  75.1 14.3 %collective-permute-start.6 = (bf16[400,512]{1,0:T(8,128)(2,1)S(1)}, bf16[400,512]{1,0:T(8,128)(2,1)S(1)}, u32[]{:S(2)}, u32[]{:S(2)}) collective-permute-start(bf16[400,512]{1,0:T(8,128)(2,1)S(1)} %attend2.1.refs_0_), channel_id=1, source_target_pairs={{0,512},{256,768},{512,0},{768,256},{1,513},{257,769},{513,1},{769... | collective-permute-start | bytes 1228808 | tf_op jit(solution)/shard_map/ppermute | solution.py:35
  79.9 10.8 %collective-permute-start.5 = (bf16[400,512]{1,0:T(8,128)(2,1)S(1)}, bf16[400,512]{1,0:T(8,128)(2,1)S(1)}, u32[]{:S(2)}, u32[]{:S(2)}) collective-permute-start(bf16[400,512]{1,0:T(8,128)(2,1)S(1)} %attend2.1.refs_0_), channel_id=1, source_target_pairs={{0,768},{256,0},{512,256},{768,512},{1,769},{257,1},{513,257},{769... | collective-permute-start | bytes 1228808 | tf_op jit(solution)/shard_map/ppermute | solution.py:35

commit v6 on v5

--- a/solution.py
+++ b/solution.py
@@ -174,7 +174,7 @@
         levels.append((packed[:8] + pltpu.roll(packed[:8], 4, 0)) + packed[8:])
     top = functools.reduce(jnp.maximum, levels)
     terms = [jnp.exp2(level - top) for level in levels]
-    total = (terms[0] + terms[2]) + (terms[1] + terms[3])
+    total = (terms[0] + terms[1]) + (terms[2] + terms[3])
     shares = [term / total for term in terms]
     blank = jnp.zeros((LANES - 8 * len(parts), rows), jnp.float32)
     shares = jnp.transpose(jnp.concatenate(shares + [blank], axis=0))
@@ -184,7 +184,7 @@
             part[:rows, cols].astype(jnp.float32) * shares[:, 8 * i + h : 8 * i + h + 1]
             for i, part in enumerate(parts)
         ]
-        out_ref[:, cols] = ((terms[0] + terms[2]) + (terms[1] + terms[3])).astype(jnp.bfloat16)
+        out_ref[:, cols] = ((terms[0] + terms[1]) + (terms[2] + terms[3])).astype(jnp.bfloat16)
 
 
 def params():
@@ -258,7 +258,7 @@
         chunks = [arrived[arrival] for arrival in arrivals]
         state = stage_call(factor, size, key_rows, stage, begin, queries, state, chunks)
     part = state
-    parts = [part] + [shift(part, "section", by, splits) for by in reversed(range(1, splits))]
+    parts = [part] + [shift(part, "section", by, splits) for by in (2, 3, 1)]
     return merge_call(size, rows, parts)
 
 

time: 93.9 us -> 93.1 us (level)
  transfers between devices with their start and end apart: 8 -> 8, of which waited for: 7 -> 6; matrix products, arithmetic and copies ran while one was open for 0% -> 0% of each run, Pallas kernels for 6% -> 6%
where the time goes in v6:
time: 93.1 us; the launch traced here: 92.5 us
  waiting for transfers between devices  41.6 us (45%)
  starting transfers between devices  40.8 us (44%)
  Pallas kernels  9.03 us (10%)
    ppermute x8, waiting for transfers between devices, shift(): lax.ppermute(value, axis, [(i, (i + by) % count) for i in range(count)])  41.6 us
    ppermute x8, starting transfers between devices, shift(): lax.ppermute(value, axis, [(i, (i + by) % count) for i in range(count)])  40.8 us
    pallas_call x3, Pallas kernels, stage_call(): pl.pallas_call(functools.partial(stage_kernel, factor, size, key_rows, st...  6.52 us
  transfers between devices with their start and end apart: 8, of which 6 were waited for; matrix products, arithmetic and copies ran while one was open for 0% of the time, Pallas kernels for 6%

profile of v6, /device:TPU:6, one launch (start us, length us, event | category | flops | bytes accessed | tf_op | source)
XLA Modules:
  0.0 92.5 jit_solution(9903070331903776923)
XLA Ops:
  0.0 11.9 %collective-permute-start = (bf16[96,256]{1,0:T(8,128)(2,1)}, bf16[96,256]{1,0:T(8,128)(2,1)S(1)}, u32[]{:S(2)}, u32[]{:S(2)}) collective-permute-start(bf16[96,256]{1,0:T(8,128)(2,1)} %bitcast.1), channel_id=1, source_target_pairs={{0,6},{1,7},{2,8},{3,9},{4,10},{5,11},{6,12},{7,13},{8,14},{9,15},... | collective-permute-start | bytes 147464 | tf_op jit(solution)/shard_map/ppermute | solution.py:35
  11.9 12.7 %collective-permute-done.refs_1_ = bf16[96,256]{1,0:T(8,128)(2,1)S(1)} collective-permute-done((bf16[96,256]{1,0:T(8,128)(2,1)}, bf16[96,256]{1,0:T(8,128)(2,1)S(1)}, u32[]{:S(2)}, u32[]{:S(2)}) %collective-permute-start) | collective-permute-done | bytes 49184 | tf_op jit(solution)/shard_map/ppermute | solution.py:35
  24.6 4.2 %collective-permute-start.1 = (bf16[96,256]{1,0:T(8,128)(2,1)S(1)}, bf16[96,256]{1,0:T(8,128)(2,1)S(1)}, u32[]{:S(2)}, u32[]{:S(2)}) collective-permute-start(bf16[96,256]{1,0:T(8,128)(2,1)S(1)} %collective-permute-done.refs_1_), channel_id=1, source_target_pairs={{0,6},{1,7},{2,8},{3,9},{4,10},{5,11},{6,12},{7,13},{8,14},{9,15},... | collective-permute-start | bytes 147464 | tf_op jit(solution)/shard_map/ppermute | solution.py:35
  28.8 10.0 %collective-permute-done.1.refs_2_ = bf16[96,256]{1,0:T(8,128)(2,1)S(1)} collective-permute-done((bf16[96,256]{1,0:T(8,128)(2,1)S(1)}, bf16[96,256]{1,0:T(8,128)(2,1)S(1)}, u32[]{:S(2)}, u32[]{:S(2)}) %collective-permute-start.1) | collective-permute-done | bytes 49184 | tf_op jit(solution)/shard_map/ppermute | solution.py:35
  38.8 0.8 pad_maximum_fusion.1
  39.6 0.0 copy-start.1
  39.6 6.7 %collective-permute-start.2 = (bf16[288,256]{1,0:T(8,128)(2,1)S(1)}, bf16[288,256]{1,0:T(8,128)(2,1)S(1)}, u32[]{:S(2)}, u32[]{:S(2)}) collective-permute-start(bf16[288,256]{1,0:T(8,128)(2,1)S(1)} %pad_maximum_fusion.1), channel_id=1, source_target_pairs={{0,3},{1,4},{2,5},{3,6},{4,7},{5,8},{6,9},{7,10},{8,11},{9,12},{10... | collective-permute-start | bytes 442376 | tf_op jit(solution)/shard_map/ppermute | solution.py:35
  46.4 0.0 copy-done.2
  46.4 0.7 bounds.1.begin_ref
  47.1 1.6 %attend0.1 = (f32[384,512]{1,0:T(8,128)S(1)}, f32[384,512]{1,0:T(8,128)S(1)}, f32[384,128]{1,0:T(8,128)S(1)}) custom-call(s32[384,128]{1,0:T(8,128)S(1)} %bounds.1.begin_ref, bf16[384,512]{1,0:T(8,128)(2,1)S(1)} %copy-done, bf16[96,256]{1,0:T(8,128)(2,1)S(1)} %bitcast.3, bf16[96,256]{1,0:T(8,128)(2,1)S(1)} %collective-permute-done.refs_1_, ...), custom_call_target="tpu_custom_call" | custom-call | flops 226492416 | bytes 393216 | tf_op jit(solution)/shard_map/attend0/pallas_call | solution.py:214
  48.7 8.1 %collective-permute-done.2.refs_3_ = bf16[288,256]{1,0:T(8,128)(2,1)S(1)} collective-permute-done((bf16[288,256]{1,0:T(8,128)(2,1)S(1)}, bf16[288,256]{1,0:T(8,128)(2,1)S(1)}, u32[]{:S(2)}, u32[]{:S(2)}) %collective-permute-start.2) | collective-permute-done | bytes 147488 | tf_op jit(solution)/shard_map/ppermute | solution.py:35
  56.8 1.9 %collective-permute-start.3 = (bf16[576,256]{1,0:T(8,128)(2,1)S(1)}, bf16[576,256]{1,0:T(8,128)(2,1)S(1)}, u32[]{:S(2)}, u32[]{:S(2)}) collective-permute-start(bf16[576,256]{1,0:T(8,128)(2,1)S(1)} %pad_maximum_fusion), channel_id=1, source_target_pairs={{0,1},{1,2},{2,3},{3,4},{4,5},{5,6},{6,7},{7,8},{8,9},{9,10},{10,1... | collective-permute-start | bytes 884744 | tf_op jit(solution)/shard_map/ppermute | solution.py:35
  58.8 5.1 %collective-permute-start.4 = (bf16[480,256]{1,0:T(8,128)(2,1)S(1)}, bf16[480,256]{1,0:T(8,128)(2,1)S(1)}, u32[]{:S(2)}, u32[]{:S(2)}) collective-permute-start(bf16[480,256]{1,0:T(8,128)(2,1)S(1)} %slice.3), channel_id=1, source_target_pairs={{0,31},{1,0},{2,1},{3,2},{4,3},{5,4},{6,5},{7,6},{8,7},{9,8},{10,9... | collective-permute-start | bytes 737288 | tf_op jit(solution)/shard_map/ppermute | solution.py:35
  63.9 2.7 %collective-permute-done.3.refs_4_ = bf16[576,256]{1,0:T(8,128)(2,1)S(1)} collective-permute-done((bf16[576,256]{1,0:T(8,128)(2,1)S(1)}, bf16[576,256]{1,0:T(8,128)(2,1)S(1)}, u32[]{:S(2)}, u32[]{:S(2)}) %collective-permute-start.3) | collective-permute-done | bytes 294944 | tf_op jit(solution)/shard_map/ppermute | solution.py:35
  66.7 2.8 %attend1.1 = (f32[384,512]{1,0:T(8,128)S(1)}, f32[384,512]{1,0:T(8,128)S(1)}, f32[384,128]{1,0:T(8,128)S(1)}) custom-call(s32[384,128]{1,0:T(8,128)S(1)} %bounds.1.begin_ref, bf16[384,512]{1,0:T(8,128)(2,1)S(1)} %copy-done, f32[384,512]{1,0:T(8,128)S(1)} %get-tuple-element.18.refs_0_, f32[384,512]{1,0:T(8,128)S(1)} %get-tuple-element.19.refs_1_, ...), custom_call_target="tpu_custom_call" | custom-call | flops 679477248 | bytes 393216 | tf_op jit(solution)/shard_map/attend1/pallas_call | solution.py:214
  69.5 0.0 collective-permute-done.4.refs_3_
  69.5 2.0 %attend2.1.refs_0_ = bf16[400,512]{1,0:T(8,128)(2,1)S(1)} custom-call(s32[384,128]{1,0:T(8,128)S(1)} %bounds.1.begin_ref, bf16[384,512]{1,0:T(8,128)(2,1)S(1)} %copy-done, f32[384,512]{1,0:T(8,128)S(1)} %get-tuple-element.22.refs_0_, f32[384,512]{1,0:T(8,128)S(1)} %get-tuple-element.23.refs_1_, f32[384,128]{1,0:T(8,128)S(1)} %get-tuple-element.24.refs_2_, ...), custom_call_target="tpu_custom_call" | custom-call | flops 377487360 | bytes 393216 | tf_op jit(solution)/shard_map/attend2/pallas_call | solution.py:214
  71.6 3.5 %collective-permute-start.7 = (bf16[400,512]{1,0:T(8,128)(2,1)S(1)}, bf16[400,512]{1,0:T(8,128)(2,1)S(1)}, u32[]{:S(2)}, u32[]{:S(2)}) collective-permute-start(bf16[400,512]{1,0:T(8,128)(2,1)S(1)} %attend2.1.refs_0_), channel_id=1, source_target_pairs={{0,256},{256,512},{512,768},{768,0},{1,257},{257,513},{513,769},{7... | collective-permute-start | bytes 1228808 | tf_op jit(solution)/shard_map/ppermute | solution.py:35
  75.1 3.6 %collective-permute-start.6 = (bf16[400,512]{1,0:T(8,128)(2,1)S(1)}, bf16[400,512]{1,0:T(8,128)(2,1)S(1)}, u32[]{:S(2)}, u32[]{:S(2)}) collective-permute-start(bf16[400,512]{1,0:T(8,128)(2,1)S(1)} %attend2.1.refs_0_), channel_id=1, source_target_pairs={{0,768},{256,0},{512,256},{768,512},{1,769},{257,1},{513,257},{769... | collective-permute-start | bytes 1228808 | tf_op jit(solution)/shard_map/ppermute | solution.py:35
  78.6 3.9 %collective-permute-start.5 = (bf16[400,512]{1,0:T(8,128)(2,1)S(1)}, bf16[400,512]{1,0:T(8,128)(2,1)S(1)}, u32[]{:S(2)}, u32[]{:S(2)}) collective-permute-start(bf16[400,512]{1,0:T(8,128)(2,1)S(1)} %attend2.1.refs_0_), channel_id=1, source_target_pairs={{0,512},{256,768},{512,0},{768,256},{1,513},{257,769},{513,1},{769... | collective-permute-start | bytes 1228808 | tf_op jit(solution)/shard_map/ppermute | solution.py:35
  82.5 3.7 %collective-permute-done.7.refs_3_ = bf16[400,512]{1,0:T(8,128)(2,1)S(1)} collective-permute-done((bf16[400,512]{1,0:T(8,128)(2,1)S(1)}, bf16[400,512]{1,0:T(8,128)(2,1)S(1)}, u32[]{:S(2)}, u32[]{:S(2)}) %collective-permute-start.7) | collective-permute-done | bytes 409632 | tf_op jit(solution)/shard_map/ppermute | solution.py:35
  86.2 0.0 collective-permute-done.6.refs_2_
  86.2 4.4 %collective-permute-done.5.refs_1_ = bf16[400,512]{1,0:T(8,128)(2,1)S(1)} collective-permute-done((bf16[400,512]{1,0:T(8,128)(2,1)S(1)}, bf16[400,512]{1,0:T(8,128)(2,1)S(1)}, u32[]{:S(2)}, u32[]{:S(2)}) %collective-permute-start.5) | collective-permute-done | bytes 409632 | tf_op jit(solution)/shard_map/ppermute | solution.py:35
  90.6 1.8 %merge.1 = bf16[384,512]{1,0:T(8,128)(2,1)} custom-call(bf16[400,512]{1,0:T(8,128)(2,1)S(1)} %attend2.1.refs_0_, bf16[400,512]{1,0:T(8,128)(2,1)S(1)} %collective-permute-done.5.refs_1_, bf16[400,512]{1,0:T(8,128)(2,1)S(1)} %collective-permute-done.6.refs_2_, bf16[400,512]{1,0:T(8,128)(2,1)S(1)} %collective-permute-done.7.refs_3_), custom_call_target="tpu_custom_call" | custom-call | tf_op jit(solution)/shard_map/merge/pallas_call | solution.py:227
  (6 shorter events, 0.0 us)
Async XLA Ops:
  0.0 46.4 %copy-start.2 = (s32[8]{0:T(128)S(1)}, s32[8]{0:T(128)}, u32[]{:S(2)}) copy-start(s32[8]{0:T(128)} %lengths.1) | copy-start | bytes 100
  0.0 47.1 %copy-start = (bf16[384,512]{1,0:T(8,128)(2,1)S(1)}, bf16[384,512]{1,0:T(8,128)(2,1)}, u32[]{:S(2)}) copy-start(bf16[384,512]{1,0:T(8,128)(2,1)} %q_ref.5) | copy-start | bytes 1179652
  0.0 24.6 %collective-permute-start = (bf16[96,256]{1,0:T(8,128)(2,1)}, bf16[96,256]{1,0:T(8,128)(2,1)S(1)}, u32[]{:S(2)}, u32[]{:S(2)}) collective-permute-start(bf16[96,256]{1,0:T(8,128)(2,1)} %bitcast.1), channel_id=1, source_target_pairs={{0,6},{1,7},{2,8},{3,9},{4,10},{5,11},{6,12},{7,13},{8,14},{9,15},... | collective-permute-start | bytes 147464 | tf_op jit(solution)/shard_map/ppermute | solution.py:35
  24.6 14.2 %collective-permute-start.1 = (bf16[96,256]{1,0:T(8,128)(2,1)S(1)}, bf16[96,256]{1,0:T(8,128)(2,1)S(1)}, u32[]{:S(2)}, u32[]{:S(2)}) collective-permute-start(bf16[96,256]{1,0:T(8,128)(2,1)S(1)} %collective-permute-done.refs_1_), channel_id=1, source_target_pairs={{0,6},{1,7},{2,8},{3,9},{4,10},{5,11},{6,12},{7,13},{8,14},{9,15},... | collective-permute-start | bytes 147464 | tf_op jit(solution)/shard_map/ppermute | solution.py:35
  39.6 7.5 %copy-start.1 = (bf16[1,1,96,1,256]{4,2,3,1,0:T(8,128)(2,1)S(1)}, bf16[1,1,96,1,256]{4,2,3,1,0:T(8,128)(2,1)}, u32[]{:S(2)}) copy-start(bf16[1,1,96,1,256]{4,2,3,1,0:T(8,128)(2,1)} %param.4) | copy-start | bytes 147460
  39.6 17.2 %collective-permute-start.2 = (bf16[288,256]{1,0:T(8,128)(2,1)S(1)}, bf16[288,256]{1,0:T(8,128)(2,1)S(1)}, u32[]{:S(2)}, u32[]{:S(2)}) collective-permute-start(bf16[288,256]{1,0:T(8,128)(2,1)S(1)} %pad_maximum_fusion.1), channel_id=1, source_target_pairs={{0,3},{1,4},{2,5},{3,6},{4,7},{5,8},{6,9},{7,10},{8,11},{9,12},{10... | collective-permute-start | bytes 442376 | tf_op jit(solution)/shard_map/ppermute | solution.py:35
  56.8 9.8 %collective-permute-start.3 = (bf16[576,256]{1,0:T(8,128)(2,1)S(1)}, bf16[576,256]{1,0:T(8,128)(2,1)S(1)}, u32[]{:S(2)}, u32[]{:S(2)}) collective-permute-start(bf16[576,256]{1,0:T(8,128)(2,1)S(1)} %pad_maximum_fusion), channel_id=1, source_target_pairs={{0,1},{1,2},{2,3},{3,4},{4,5},{5,6},{6,7},{7,8},{8,9},{9,10},{10,1... | collective-permute-start | bytes 884744 | tf_op jit(solution)/shard_map/ppermute | solution.py:35
  58.8 10.7 %collective-permute-start.4 = (bf16[480,256]{1,0:T(8,128)(2,1)S(1)}, bf16[480,256]{1,0:T(8,128)(2,1)S(1)}, u32[]{:S(2)}, u32[]{:S(2)}) collective-permute-start(bf16[480,256]{1,0:T(8,128)(2,1)S(1)} %slice.3), channel_id=1, source_target_pairs={{0,31},{1,0},{2,1},{3,2},{4,3},{5,4},{6,5},{7,6},{8,7},{9,8},{10,9... | collective-permute-start | bytes 737288 | tf_op jit(solution)/shard_map/ppermute | solution.py:35
  71.6 14.7 %collective-permute-start.7 = (bf16[400,512]{1,0:T(8,128)(2,1)S(1)}, bf16[400,512]{1,0:T(8,128)(2,1)S(1)}, u32[]{:S(2)}, u32[]{:S(2)}) collective-permute-start(bf16[400,512]{1,0:T(8,128)(2,1)S(1)} %attend2.1.refs_0_), channel_id=1, source_target_pairs={{0,256},{256,512},{512,768},{768,0},{1,257},{257,513},{513,769},{7... | collective-permute-start | bytes 1228808 | tf_op jit(solution)/shard_map/ppermute | solution.py:35
  75.1 11.2 %collective-permute-start.6 = (bf16[400,512]{1,0:T(8,128)(2,1)S(1)}, bf16[400,512]{1,0:T(8,128)(2,1)S(1)}, u32[]{:S(2)}, u32[]{:S(2)}) collective-permute-start(bf16[400,512]{1,0:T(8,128)(2,1)S(1)} %attend2.1.refs_0_), channel_id=1, source_target_pairs={{0,768},{256,0},{512,256},{768,512},{1,769},{257,1},{513,257},{769... | collective-permute-start | bytes 1228808 | tf_op jit(solution)/shard_map/ppermute | solution.py:35
  78.6 12.0 %collective-permute-start.5 = (bf16[400,512]{1,0:T(8,128)(2,1)S(1)}, bf16[400,512]{1,0:T(8,128)(2,1)S(1)}, u32[]{:S(2)}, u32[]{:S(2)}) collective-permute-start(bf16[400,512]{1,0:T(8,128)(2,1)S(1)} %attend2.1.refs_0_), channel_id=1, source_target_pairs={{0,512},{256,768},{512,0},{768,256},{1,513},{257,769},{513,1},{769... | collective-permute-start | bytes 1228808 | tf_op jit(solution)/shard_map/ppermute | solution.py:35
